TPU v7x, 512 devices: a whole 4x4x16 slice. The times are simulated.
512 devices in a mesh: row: 32 (over y, z_lo), col: 16 (over z_hi, x, core).
Axes of the slice: x: 4, y: 4, z: 16 (z_hi: 2, z_lo: 8; z = z_hi * 8 + z_lo), core: 2. Of those that a mesh axis runs over, the one named last changes fastest.
Arguments:
- inverse_block: bfloat16 [20480, 20480], P('row', 'col'), may hold values from -0.078125 to 0.078125
- lower_panel: bfloat16 [20480, 2, 384], P(('row', 'col')), may hold values from -0.75 to 0.75
- structure: int32 [160, 2], replicated, may hold values 0 or 1
- diag_inverse: float32 [2, 384, 384], P(None, 'row'), may hold values from -6 to 6
Outputs:
- inverse_panel: bfloat16 [20480, 2, 384], P(('row', 'col'))
- diag_block: float32 [2, 384, 384], P(None, 'row')
Inputs may be any that keep to these rules, and one draw needn't show every extreme that they name: `structure`: 1 where the block of rows belongs to the panel.
All inputs are finite; a program needn't handle non-finite values.
Results may differ from a plain program's by a relative error of at most 0.013.
Values may be sent and summed in bfloat16 or wider, within the bound.
No kernel may reach another device: no remote copies, remote signals or barrier semaphores. Data moves between devices by JAX's collectives and lax.ppermute only.
A program may use at most 64 MiB of HBM per device.

v0:
```python
import jax
import jax.numpy as jnp
from jax import lax
from jax.sharding import PartitionSpec as P

BS = 128


def passed_along(block, axis, distance):
    devices = range(lax.axis_size(axis))
    route = [(i - distance, i) for i in devices if i - distance in devices]
    return lax.ppermute(block, axis, route)


def spread(x, axis, root):
    mine = lax.axis_index(axis) == root
    return lax.psum(jnp.where(mine, x, jnp.zeros_like(x)), axis)


def fetch_columns(piece):
    near_rows = lax.all_gather(piece, "col", axis=0, tiled=True)
    col_id = lax.axis_index("col")
    lower_half = passed_along(near_rows, "row", 1)
    paired = jnp.concatenate([lower_half, near_rows], axis=0)
    return spread(paired, "row", 2 * col_id + 1)


def sum_blocks(inverse_block, piece):
    columns = fetch_columns(piece)
    return lax.psum_scatter(
        jnp.dot(inverse_block, columns, preferred_element_type=jnp.float32),
        "col",
        scatter_dimension=0,
        tiled=True,
    )


def shards(inverse_block, lower_panel, structure, diag_inverse):
    row_count = lower_panel.shape[0]
    panel_count = lower_panel.shape[1]
    flat_index = lax.axis_index("row") * lax.axis_size("col") + lax.axis_index("col")
    global_rows = flat_index * row_count + lax.iota(jnp.int32, row_count)
    block_ids = global_rows // BS
    onehot = (
        block_ids[:, None] == jnp.arange(structure.shape[0], dtype=jnp.int32)[None, :]
    ).astype(jnp.float32)
    keep_rows = jnp.dot(onehot, structure.astype(jnp.float32))
    masked = lower_panel * keep_rows[:, :, None].astype(jnp.bfloat16)
    product = jnp.stack(
        [sum_blocks(inverse_block, masked[:, panel_id, :]) for panel_id in range(panel_count)],
        axis=1,
    )
    inverse_panel = (-product).astype(jnp.bfloat16)
    schur_part = jnp.einsum(
        "rpi,rpj->pij", masked.astype(jnp.float32), product, precision=lax.Precision.HIGHEST
    )
    strip_rows = diag_inverse.shape[1]
    schur_total = lax.psum(schur_part, ("row", "col"))
    schur_local = lax.dynamic_slice_in_dim(
        schur_total, lax.axis_index("row") * strip_rows, strip_rows, 1
    )
    return (inverse_panel, diag_inverse + schur_local)


def solution(mesh):
    return jax.shard_map(
        shards,
        mesh=mesh,
        in_specs=(P("row", "col"), P(("row", "col"), None, None), P(), P(None, "row", None)),
        out_specs=(P(("row", "col"), None, None), P(None, "row", None)),
        check_vma=False,
    )
```

profile of v0, /device:TPU:1, one launch (start us, length us, event | category | flops | bytes accessed | tf_op | source)
XLA Modules:
  0.0 1341.0 jit_solution(6422971746933503226)
XLA Ops:
  7.2 0.0 copy-start
  7.2 0.0 all-reduce.12.cloned.1.call-start
  7.2 1.0 convolution_convert_fusion
  8.2 0.9 copy_multiply_fusion
  9.2 52.3 %all-gather = bf16[640,1,384]{2,0,1:T(8,128)(2,1)S(1)} all-gather(bf16[40,1,384]{2,0,1:T(8,128)(2,1)S(1)} %get-tuple-element.12), channel_id=2, replica_groups=mesh['row'=32,'col'=16] {'col'}, dimensions={0}, use_global_device_ids=true | all-gather | bytes 522240 | tf_op jit(solution)/shard_map/all_gather | solution.py:21
  61.4 2.6 collective-permute-start
  64.1 46.1 %all-gather.1 = bf16[640,1,384]{2,0,1:T(8,128)(2,1)S(1)} all-gather(bf16[40,1,384]{2,0,1:T(8,128)(2,1)S(1)} %get-tuple-element.13), channel_id=3, replica_groups=mesh['row'=32,'col'=16] {'col'}, dimensions={0}, use_global_device_ids=true | all-gather | bytes 522240 | tf_op jit(solution)/shard_map/all_gather | solution.py:21
  110.2 2.1 collective-permute-start.1
  112.3 0.0 collective-permute-done
  112.3 1.2 maximum_select_fusion
  113.4 8.7 collective-permute-done.1
  122.1 2.2 maximum_select_fusion.1
  124.3 0.0 all-reduce.12.cloned.1.call-update
  124.3 0.0 all-reduce.10.cloned.1.call-start
  124.4 439.7 %all-reduce.12.cloned.1.call-done = (bf16[1280,384]{1,0:T(8,128)(2,1)}, bf16[1280,384]{1,0:T(8,128)(2,1)}) async-done(((bf16[1280,384]{1,0:T(8,128)(2,1)}, bf16[1280,384]{1,0:T(8,128)(2,1)}), (bf16[1280,384]{1,0:T(8,128)(2,1)}, bf16[1280,384]{1,0:T(8,128)(2,1)})) %all-reduce.12.cloned.1.call-update) | async-done | bytes 1966096 | tf_op jit(solution)/shard_map/psum | solution.py:17
  564.0 0.0 copy-done
  564.0 3.2 convolution_bitcast_fusion
  567.2 2.0 convolution_bitcast_fusion.1
  569.2 0.0 all-reduce.10.cloned.1.call-update
  569.2 0.0 all-reduce.8.cloned.1.call-start
  569.3 1.3 dynamic-slice
  571.2 286.1 %all-reduce.10.cloned.1.call-done = (f32[640,384]{0,1:T(8,128)}, f32[640,384]{0,1:T(8,128)}) async-done(((f32[640,384]{0,1:T(8,128)}, f32[640,384]{0,1:T(8,128)}), (f32[640,384]{0,1:T(8,128)}, f32[640,384]{0,1:T(8,128)})) %all-reduce.10.cloned.1.call-update) | async-done | bytes 1966096
  857.3 1.3 dynamic-slice_bitcast_fusion
  858.6 0.0 copy-start.1
  858.6 0.1 copy.19
  858.7 0.1 copy.20
  858.8 1.7 fusion
  860.5 0.0 all-reduce.8.cloned.1.call-update
  860.6 0.7 copy.22
  861.2 471.7 %all-reduce.8.cloned.1.call-done = f32[2,384,384]{2,1,0:T(8,128)} async-done(((f32[2,384,384]{2,1,0:T(8,128)}), f32[2,384,384]{2,1,0:T(8,128)}) %all-reduce.8.cloned.1.call-update) | async-done | bytes 1179664 | tf_op jit(solution)/shard_map/psum | solution.py:58
  1332.9 0.9 copy_add_fusion
  1333.8 0.6 copy.23
  (6 shorter events, 0.0 us)
Async XLA Ops:
  7.2 556.9 %copy-start = (bf16[640,1280]{1,0:T(8,128)(2,1)S(1)}, bf16[640,1280]{1,0:T(8,128)(2,1)}, u32[]{:S(2)}) copy-start(bf16[640,1280]{1,0:T(8,128)(2,1)} %param.4) | copy-start | bytes 4915204
  7.2 556.9 %all-reduce.12.cloned.1.call-start = ((), (), s32[]{:S(2)}) async-start(), calls=%async_computation.2 | async-start | bytes 3932160 | tf_op jit(solution)/shard_map/psum | solution.py:17
  61.4 50.8 %collective-permute-start = (bf16[640,384]{1,0:T(8,128)(2,1)S(1)}, bf16[640,384]{1,0:T(8,128)(2,1)S(1)}, u32[]{:S(2)}, u32[]{:S(2)}) collective-permute-start(bf16[640,384]{1,0:T(8,128)(2,1)S(1)} %bitcast.20), channel_id=1, source_target_pairs={{0,16},{16,32},{32,48},{48,64},{64,80},{80,96},{96,112},{112,128},... | collective-permute-start | bytes 1474568 | tf_op jit(solution)/shard_map/ppermute | solution.py:12
  110.2 12.0 collective-permute-start.1
  124.3 733.0 %all-reduce.10.cloned.1.call-start = ((), (), s32[]{:S(2)}) async-start(), calls=%async_computation.1 | async-start | bytes 3932160
  564.0 3.2 copy-start.2
  569.2 763.7 %all-reduce.8.cloned.1.call-start = ((), (), s32[]{:S(2)}) async-start(), calls=%async_computation | async-start | bytes 2359296 | tf_op jit(solution)/shard_map/psum | solution.py:58
  858.6 474.3 %copy-start.1 = (f32[2,12,384]{2,0,1:T(2,128)S(1)}, f32[2,12,384]{2,0,1:T(2,128)}, u32[]{:S(2)}) copy-start(f32[2,12,384]{2,0,1:T(2,128)} %param.7) | copy-start | bytes 110596
Sparse Core Ops, SparseCore 0:
  124.4 439.5 all-reduce.11
  569.3 287.9 all-reduce.9
  862.7 470.1 all-reduce.7
where the time goes:
time: 1340 us
  waiting for transfers between devices  1210 us (90%)
  blocking collectives  98.3 us (7%)
  between operations  14.5 us (1%)
    psum x1, waiting for transfers between devices, shards(): schur_total = lax.psum(schur_part, ('row', 'col'))  472 us
    psum x1, waiting for transfers between devices, spread(): return lax.psum(jnp.where(mine, x, jnp.zeros_like(x)), axis)  440 us
    unnamed x4, waiting for transfers between devices  286 us
    all_gather x2, blocking collectives, fetch_columns(): near_rows = lax.all_gather(piece, 'col', axis=0, tiled=True)  98.3 us
  transfers between devices with their start and end apart: 5, of which 4 were waited for; matrix products, arithmetic and copies ran while one was open for 0% of the time, Pallas kernels for 0%

commit v1 on v0

v1 whole, which is shorter than its diff:
```python
import jax
import jax.numpy as jnp
from jax import lax
from jax.sharding import Mesh, PartitionSpec as P

BS = 128
AXES = ("y", "g", "q", "zh", "x", "k")
SIZES = (4, 2, 4, 2, 4, 2)
ROW = ("y", "g", "q")
COL = ("zh", "x", "k")


def swapped(x, axis):
    return lax.ppermute(x, axis, [(0, 1), (1, 0)])


def to_columns():
    route = []
    for row in range(32):
        for col in range(16):
            zh, x, k = col // 8, (col // 2) % 4, col % 2
            target_row = ((row % 2) * 2 + zh) * 8 + k * 4 + x
            route.append((row * 16 + col, target_row * 16 + row // 2))
    return route


def gathered(x, axis):
    n = lax.axis_size(axis)
    return lax.all_to_all(jnp.broadcast_to(x[None], (n,) + x.shape), axis, 0, 0)


def ordered(mine, other, index):
    first = jnp.where(index == 0, mine, other)
    second = jnp.where(index == 0, other, mine)
    return jnp.stack([first, second])


def masked_rows(lower_panel, structure):
    rows = lower_panel.shape[0]
    start = (lax.axis_index(ROW) * 16 + lax.axis_index(COL)) * rows
    block_ids = (start + lax.iota(jnp.int32, rows)) // BS
    onehot = (block_ids[:, None] == lax.iota(jnp.int32, structure.shape[0])[None, :]).astype(jnp.float32)
    keep = jnp.dot(onehot, structure.astype(jnp.float32))
    return lower_panel * keep[:, :, None].astype(jnp.bfloat16)


def added(parts):
    return jnp.sum(parts.astype(jnp.float32), axis=0)


def shards(inverse_block, lower_panel, structure, diag_inverse):
    f32, bf16 = jnp.float32, jnp.bfloat16
    k = lax.axis_index("k")
    zh = lax.axis_index("zh")
    flat = masked_rows(lower_panel, structure).reshape(40, 768)

    pair = ordered(flat, swapped(flat, "k"), k)
    moved = lax.ppermute(pair, AXES, to_columns())
    quarter = gathered(moved.reshape(80, 768), "q").reshape(320, 768)
    own_rows = jnp.where(k == 0, pair[..., :384], pair[..., 384:])
    quarter, own_rows = lax.optimization_barrier((quarter, own_rows))
    columns = gathered(quarter, "y").reshape(1280, 768)
    far_rows = swapped(own_rows, "zh")
    columns, far_rows = lax.optimization_barrier((columns, far_rows))

    product = jnp.dot(inverse_block, columns, preferred_element_type=f32)

    mine = jnp.where(k == 0, product[:, :384], product[:, 384:])
    sent = jnp.where(k == 0, product[:, 384:], product[:, :384]).astype(bf16)
    summed = (mine + swapped(sent, "k").astype(f32)).astype(bf16)
    chunks = summed.reshape(2, 4, 80, 384).transpose(1, 0, 2, 3)
    near = added(lax.all_to_all(chunks, "x", 0, 0))
    near_b = near.astype(bf16)

    rows = ordered(own_rows, far_rows, zh).reshape(160, 384)
    schur = lax.dot_general(
        rows, near_b.reshape(160, 384), (((0,), (0,)), ((), ())), preferred_element_type=f32
    ).astype(bf16)

    by_yq = schur.reshape(4, 2, 4, 12, 384).transpose(0, 2, 1, 3, 4)
    by_yq = added(lax.all_to_all(by_yq.reshape(16, 2, 12, 384), ("y", "q"), 0, 0)).astype(bf16)

    near_b = near_b.reshape(2, 2, 40, 384)
    kept = jnp.where(k == 0, near_b[:, 0], near_b[:, 1])
    other = swapped(jnp.where(k == 0, near_b[:, 1], near_b[:, 0]), "k")
    halves = jnp.stack([jnp.where(k == 0, kept, other), jnp.where(k == 0, other, kept)], axis=1)
    halves, by_yq = lax.optimization_barrier((halves, by_yq))
    by_z = jnp.broadcast_to(by_yq[:, None], (2, 2, 12, 384)).reshape(4, 12, 384)
    by_z = added(lax.all_to_all(by_z, ("g", "zh"), 0, 0)).astype(bf16)
    far_half = swapped(jnp.where(zh == 0, halves[1], halves[0]), "zh").astype(f32)
    own_half = jnp.where(zh == 0, halves[0], halves[1]).astype(f32)
    inverse_panel = (-(own_half + far_half)).astype(bf16).transpose(1, 0, 2)

    total = jnp.sum(gathered(by_z, ("x", "k")).reshape(4, 2, 12, 384).astype(f32), axis=0)
    return inverse_panel, diag_inverse + total


def solution(mesh):
    fine = Mesh(mesh.devices.reshape(SIZES), AXES)
    return jax.shard_map(
        shards,
        mesh=fine,
        in_specs=(P(ROW, COL), P(AXES, None, None), P(), P(None, ROW, None)),
        out_specs=(P(AXES, None, None), P(None, ROW, None)),
        check_vma=False,
    )
```

time: 1340 us -> 157 us (0.12)
  waiting for transfers between devices: 1210 us -> 43 us
  blocking collectives: 98.3 us -> 0 us
  starting transfers between devices: 4.85 us -> 99.3 us
  between operations: 14.5 us -> 0.89 us
    psum x2 -> x0, waiting for transfers between devices: 911 us -> none  [the longest x1 472 us: shards(): schur_total = lax.psum(schur_part, ('row', 'col'))]
    unnamed x4 -> x0, waiting for transfers between devices: 286 us -> none
    all_gather x2 -> x0, blocking collectives: 98.3 us -> none  [fetch_columns(): near_rows = lax.all_gather(piece, 'col', axis=0, tiled=True)]
    ppermute x2 -> x6, starting transfers between devices: 4.73 us -> 54.3 us  [the longest x5 50.6 us: swapped(): return lax.ppermute(x, axis, [(0, 1), (1, 0)])]
    all_to_all x0 -> x6, starting transfers between devices: none -> 45 us  [the longest x3 18 us: gathered(): return lax.all_to_all(jnp.broadcast_to(x[None], (n,) + x.shape), axis, 0, 0)]
    all_to_all x0 -> x6, waiting for transfers between devices: none -> 33.7 us  [the longest x3 19.2 us: gathered(): return lax.all_to_all(jnp.broadcast_to(x[None], (n,) + x.shape), axis, 0, 0)]
  transfers between devices with their start and end apart: 5 -> 12, of which waited for: 4 -> 9; matrix products, arithmetic and copies ran while one was open for 0% -> 1% of each run, Pallas kernels for 0% -> 0%
where the time goes in v1:
time: 157 us; the launch traced here: 156 us
  starting transfers between devices  99.3 us (63%)
  waiting for transfers between devices  43 us (27%)
  local copies, waits for them, and re-layouts  6.92 us (4%)
  matrix products  4.26 us (3%)
  other arithmetic  1.82 us (1%)
    ppermute x5, starting transfers between devices, swapped(): return lax.ppermute(x, axis, [(0, 1), (1, 0)])  50.6 us
    all_to_all x3, waiting for transfers between devices, gathered(): return lax.all_to_all(jnp.broadcast_to(x[None], (n,) + x.shape), axis, 0, 0)  19.2 us
    all_to_all x3, starting transfers between devices, gathered(): return lax.all_to_all(jnp.broadcast_to(x[None], (n,) + x.shape), axis, 0, 0)  18 us
    all_to_all x1, starting transfers between devices, shards(): near = added(lax.all_to_all(chunks, 'x', 0, 0))  13.7 us
    all_to_all x1, starting transfers between devices, shards(): by_z = added(lax.all_to_all(by_z, ('g', 'zh'), 0, 0)).astype(bf16)  9.67 us
    all_to_all x1, waiting for transfers between devices, shards(): near = added(lax.all_to_all(chunks, 'x', 0, 0))  8.51 us
    all_to_all x1, waiting for transfers between devices, shards(): lax.all_to_all(by_yq.reshape(16, 2, 12, 384), ('y', 'q'), 0, 0)  5.96 us
    ppermute x5, waiting for transfers between devices, swapped(): return lax.ppermute(x, axis, [(0, 1), (1, 0)])  4.91 us
  transfers between devices with their start and end apart: 12, of which 9 were waited for; matrix products, arithmetic and copies ran while one was open for 1% of the time, Pallas kernels for 0%

profile of v1, /device:TPU:1, one launch (start us, length us, event | category | flops | bytes accessed | tf_op | source)
XLA Modules:
  0.0 156.2 jit_solution(13123101822420741859)
XLA Ops:
  0.7 1.0 convolution_convert_fusion.1
  1.8 1.0 broadcast_multiply_fusion
  2.8 8.8 %collective-permute-start = (bf16[40,768]{1,0:T(8,128)(2,1)S(1)}, bf16[40,768]{1,0:T(8,128)(2,1)S(1)}, u32[]{:S(2)}, u32[]{:S(2)}) collective-permute-start(bf16[40,768]{1,0:T(8,128)(2,1)S(1)} %bitcast.88), channel_id=1, source_target_pairs={{0,1},{1,0},{2,3},{3,2},{4,5},{5,4},{6,7},{7,6},{8,9},{9,8},{10,11... | collective-permute-start | bytes 184328 | tf_op jit(solution)/shard_map/ppermute | solution.py:14
  11.6 0.9 collective-permute-done
  12.5 3.7 %collective-permute-start.1 = (bf16[2,40,768]{2,1,0:T(8,128)(2,1)S(1)}, bf16[2,40,768]{2,1,0:T(8,128)(2,1)S(1)}, u32[]{:S(2)}, u32[]{:S(2)}) collective-permute-start(bf16[2,40,768]{2,1,0:T(8,128)(2,1)S(1)} %pad_maximum_fusion), channel_id=1, source_target_pairs={{0,0},{1,64},{2,16},{3,80},{4,32},{5,96},{6,48},{7,112},{8,128},{9... | collective-permute-start | bytes 368648 | tf_op jit(solution)/shard_map/ppermute | solution.py:58
  16.2 4.5 %collective-permute-done.1 = bf16[2,40,768]{2,1,0:T(8,128)(2,1)S(1)} collective-permute-done((bf16[2,40,768]{2,1,0:T(8,128)(2,1)S(1)}, bf16[2,40,768]{2,1,0:T(8,128)(2,1)S(1)}, u32[]{:S(2)}, u32[]{:S(2)}) %collective-permute-start.1) | collective-permute-done | bytes 122912 | tf_op jit(solution)/shard_map/ppermute | solution.py:58
  20.6 0.8 broadcast_in_dim.11
  21.4 3.9 %all-to-all-start = ((bf16[4,80,768]{2,1,0:T(8,128)(2,1)}), bf16[4,80,768]{2,1,0:T(8,128)(2,1)S(1)}, u32[]{:S(2)}, u32[]{:S(2)}) async-start(bf16[4,80,768]{2,1,0:T(8,128)(2,1)} %broadcast_in_dim.11), calls=%async_computation | async-start | bytes 983040 | tf_op jit(solution)/shard_map/all_to_all | solution.py:29
  25.4 14.9 %all-to-all-done = bf16[4,80,768]{2,1,0:T(8,128)(2,1)S(1)} async-done(((bf16[4,80,768]{2,1,0:T(8,128)(2,1)}), bf16[4,80,768]{2,1,0:T(8,128)(2,1)S(1)}, u32[]{:S(2)}, u32[]{:S(2)}) %all-to-all-start) | async-done | bytes 491552 | tf_op jit(solution)/shard_map/all_to_all | solution.py:29
  40.3 1.4 broadcast_in_dim.12
  41.7 7.7 %all-to-all-start.1 = ((bf16[4,320,768]{2,1,0:T(8,128)(2,1)}), bf16[4,320,768]{2,1,0:T(8,128)(2,1)}, u32[]{:S(2)}, u32[]{:S(2)}) async-start(bf16[4,320,768]{2,1,0:T(8,128)(2,1)} %broadcast_in_dim.12), calls=%async_computation.1 | async-start | bytes 3932160 | tf_op jit(solution)/shard_map/all_to_all | solution.py:29
  49.4 18.6 %collective-permute-start.2 = (bf16[2,40,384]{2,1,0:T(8,128)(2,1)S(1)}, bf16[2,40,384]{2,1,0:T(8,128)(2,1)S(1)}, u32[]{:S(2)}, u32[]{:S(2)}) collective-permute-start(bf16[2,40,384]{2,1,0:T(8,128)(2,1)S(1)} %fusion.6), channel_id=1, source_target_pairs={{0,8},{8,0},{1,9},{9,1},{2,10},{10,2},{3,11},{11,3},{4,12},{12,4},... | collective-permute-start | bytes 184328 | tf_op jit(solution)/shard_map/ppermute | solution.py:14
  68.0 1.7 %collective-permute-done.2 = bf16[2,40,384]{2,1,0:T(8,128)(2,1)S(1)} collective-permute-done((bf16[2,40,384]{2,1,0:T(8,128)(2,1)S(1)}, bf16[2,40,384]{2,1,0:T(8,128)(2,1)S(1)}, u32[]{:S(2)}, u32[]{:S(2)}) %collective-permute-start.2) | collective-permute-done | bytes 61472 | tf_op jit(solution)/shard_map/ppermute | solution.py:14
  69.7 3.0 %convolution_bitcast_fusion = f32[640,768]{1,0:T(8,128)S(1)} fusion(bf16[640,1280]{1,0:T(8,128)(2,1)S(1)} %copy-done, bf16[1280,768]{1,0:T(8,128)(2,1)} %bitcast.4), kind=kOutput, calls=%fused_computation | convolution fusion | flops 1258291200 | bytes 5570560 | tf_op jit(solution)/shard_map/dot_general | solution.py:66
  72.8 7.7 %collective-permute-start.3 = (bf16[640,384]{1,0:T(8,128)(2,1)S(1)}, bf16[640,384]{1,0:T(8,128)(2,1)S(1)}, u32[]{:S(2)}, u32[]{:S(2)}) collective-permute-start(bf16[640,384]{1,0:T(8,128)(2,1)S(1)} %select_convert_fusion), channel_id=1, source_target_pairs={{0,1},{1,0},{2,3},{3,2},{4,5},{5,4},{6,7},{7,6},{8,9},{9,8},{10,11... | collective-permute-start | bytes 1474568 | tf_op jit(solution)/shard_map/ppermute | solution.py:14
  80.5 1.5 collective-permute-done.3
  82.1 0.8 copy.109
  83.0 13.7 %all-to-all-start.2 = ((bf16[4,2,80,384]{3,2,1,0:T(8,128)(2,1)}), bf16[4,2,80,384]{3,2,1,0:T(8,128)(2,1)S(1)}, u32[]{:S(2)}, u32[]{:S(2)}) async-start(bf16[4,2,80,384]{3,2,1,0:T(8,128)(2,1)} %bitcast.79), calls=%async_computation.2 | async-start | bytes 983040 | tf_op jit(solution)/shard_map/all_to_all | solution.py:72
  96.8 8.5 %all-to-all-done.2 = bf16[4,2,80,384]{3,2,1,0:T(8,128)(2,1)S(1)} async-done(((bf16[4,2,80,384]{3,2,1,0:T(8,128)(2,1)}), bf16[4,2,80,384]{3,2,1,0:T(8,128)(2,1)S(1)}, u32[]{:S(2)}, u32[]{:S(2)}) %all-to-all-start.2) | async-done | bytes 491552 | tf_op jit(solution)/shard_map/all_to_all | solution.py:72
  105.7 1.0 copy.85
  106.7 3.5 %all-to-all-start.3 = ((bf16[16,2,12,384]{3,1,2,0:T(2,128)(2,1)}), bf16[16,2,12,384]{3,1,2,0:T(2,128)(2,1)S(1)}, u32[]{:S(2)}, u32[]{:S(2)}) async-start(bf16[16,2,12,384]{3,1,2,0:T(2,128)(2,1)} %bitcast.21), calls=%async_computation.3 | async-start | bytes 589824 | tf_op jit(solution)/shard_map/all_to_all | solution.py:81
  110.3 3.4 %collective-permute-start.4 = (bf16[2,40,384]{2,1,0:T(8,128)(2,1)S(1)}, bf16[2,40,384]{2,1,0:T(8,128)(2,1)S(1)}, u32[]{:S(2)}, u32[]{:S(2)}) collective-permute-start(bf16[2,40,384]{2,1,0:T(8,128)(2,1)S(1)} %fusion.2), channel_id=1, source_target_pairs={{0,1},{1,0},{2,3},{3,2},{4,5},{5,4},{6,7},{7,6},{8,9},{9,8},{10,11... | collective-permute-start | bytes 184328 | tf_op jit(solution)/shard_map/ppermute | solution.py:14
  113.7 0.9 collective-permute-done.4
  114.7 6.0 %all-to-all-done.3 = bf16[16,2,12,384]{3,1,2,0:T(2,128)(2,1)S(1)} async-done(((bf16[16,2,12,384]{3,1,2,0:T(2,128)(2,1)}), bf16[16,2,12,384]{3,1,2,0:T(2,128)(2,1)S(1)}, u32[]{:S(2)}, u32[]{:S(2)}) %all-to-all-start.3) | async-done | bytes 294944 | tf_op jit(solution)/shard_map/all_to_all | solution.py:81
  120.9 0.6 broadcast_in_dim.13
  121.5 9.7 %all-to-all-start.4 = ((bf16[4,12,384]{2,1,0:T(8,128)(2,1)}), bf16[4,12,384]{2,1,0:T(8,128)(2,1)S(1)}, u32[]{:S(2)}, u32[]{:S(2)}) async-start(bf16[4,12,384]{2,1,0:T(8,128)(2,1)} %bitcast.28), calls=%async_computation.4 | async-start | bytes 98304 | tf_op jit(solution)/shard_map/all_to_all | solution.py:89
  131.2 12.1 %collective-permute-start.5 = (bf16[2,40,384]{2,1,0:T(8,128)(2,1)S(1)}, bf16[2,40,384]{2,1,0:T(8,128)(2,1)S(1)}, u32[]{:S(2)}, u32[]{:S(2)}) collective-permute-start(bf16[2,40,384]{2,1,0:T(8,128)(2,1)S(1)} %fusion.3), channel_id=1, source_target_pairs={{0,8},{8,0},{1,9},{9,1},{2,10},{10,2},{3,11},{11,3},{4,12},{12,4},... | collective-permute-start | bytes 184328 | tf_op jit(solution)/shard_map/ppermute | solution.py:14
  143.3 0.6 broadcast_in_dim.14
  144.0 6.4 %all-to-all-start.5 = ((bf16[8,12,384]{2,1,0:T(8,128)(2,1)}), bf16[8,12,384]{2,1,0:T(8,128)(2,1)S(1)}, u32[]{:S(2)}, u32[]{:S(2)}) async-start(bf16[8,12,384]{2,1,0:T(8,128)(2,1)} %broadcast_in_dim.14), calls=%async_computation.5 | async-start | bytes 196608 | tf_op jit(solution)/shard_map/all_to_all | solution.py:29
  150.4 0.7 copy.95
  151.1 4.3 %all-to-all-done.5 = bf16[8,12,384]{2,1,0:T(8,128)(2,1)S(1)} async-done(((bf16[8,12,384]{2,1,0:T(8,128)(2,1)}), bf16[8,12,384]{2,1,0:T(8,128)(2,1)S(1)}, u32[]{:S(2)}, u32[]{:S(2)}) %all-to-all-start.5) | async-done | bytes 73760 | tf_op jit(solution)/shard_map/all_to_all | solution.py:29
  155.6 0.6 copy.96
  (32 shorter events, 1.4 us)
Async XLA Ops:
  0.6 69.1 %copy-start = (bf16[640,1280]{1,0:T(8,128)(2,1)S(1)}, bf16[640,1280]{1,0:T(8,128)(2,1)}, u32[]{:S(2)}) copy-start(bf16[640,1280]{1,0:T(8,128)(2,1)} %param.4) | copy-start | bytes 4915204
  2.8 9.7 %collective-permute-start = (bf16[40,768]{1,0:T(8,128)(2,1)S(1)}, bf16[40,768]{1,0:T(8,128)(2,1)S(1)}, u32[]{:S(2)}, u32[]{:S(2)}) collective-permute-start(bf16[40,768]{1,0:T(8,128)(2,1)S(1)} %bitcast.88), channel_id=1, source_target_pairs={{0,1},{1,0},{2,3},{3,2},{4,5},{5,4},{6,7},{7,6},{8,9},{9,8},{10,11... | collective-permute-start | bytes 184328 | tf_op jit(solution)/shard_map/ppermute | solution.py:14
  12.5 8.1 %collective-permute-start.1 = (bf16[2,40,768]{2,1,0:T(8,128)(2,1)S(1)}, bf16[2,40,768]{2,1,0:T(8,128)(2,1)S(1)}, u32[]{:S(2)}, u32[]{:S(2)}) collective-permute-start(bf16[2,40,768]{2,1,0:T(8,128)(2,1)S(1)} %pad_maximum_fusion), channel_id=1, source_target_pairs={{0,0},{1,64},{2,16},{3,80},{4,32},{5,96},{6,48},{7,112},{8,128},{9... | collective-permute-start | bytes 368648 | tf_op jit(solution)/shard_map/ppermute | solution.py:58
  21.4 18.9 %all-to-all-start = ((bf16[4,80,768]{2,1,0:T(8,128)(2,1)}), bf16[4,80,768]{2,1,0:T(8,128)(2,1)S(1)}, u32[]{:S(2)}, u32[]{:S(2)}) async-start(bf16[4,80,768]{2,1,0:T(8,128)(2,1)} %broadcast_in_dim.11), calls=%async_computation | async-start | bytes 983040 | tf_op jit(solution)/shard_map/all_to_all | solution.py:29
  41.7 28.0 %all-to-all-start.1 = ((bf16[4,320,768]{2,1,0:T(8,128)(2,1)}), bf16[4,320,768]{2,1,0:T(8,128)(2,1)}, u32[]{:S(2)}, u32[]{:S(2)}) async-start(bf16[4,320,768]{2,1,0:T(8,128)(2,1)} %broadcast_in_dim.12), calls=%async_computation.1 | async-start | bytes 3932160 | tf_op jit(solution)/shard_map/all_to_all | solution.py:29
  49.4 20.3 %collective-permute-start.2 = (bf16[2,40,384]{2,1,0:T(8,128)(2,1)S(1)}, bf16[2,40,384]{2,1,0:T(8,128)(2,1)S(1)}, u32[]{:S(2)}, u32[]{:S(2)}) collective-permute-start(bf16[2,40,384]{2,1,0:T(8,128)(2,1)S(1)} %fusion.6), channel_id=1, source_target_pairs={{0,8},{8,0},{1,9},{9,1},{2,10},{10,2},{3,11},{11,3},{4,12},{12,4},... | collective-permute-start | bytes 184328 | tf_op jit(solution)/shard_map/ppermute | solution.py:14
  72.8 9.2 %collective-permute-start.3 = (bf16[640,384]{1,0:T(8,128)(2,1)S(1)}, bf16[640,384]{1,0:T(8,128)(2,1)S(1)}, u32[]{:S(2)}, u32[]{:S(2)}) collective-permute-start(bf16[640,384]{1,0:T(8,128)(2,1)S(1)} %select_convert_fusion), channel_id=1, source_target_pairs={{0,1},{1,0},{2,3},{3,2},{4,5},{5,4},{6,7},{7,6},{8,9},{9,8},{10,11... | collective-permute-start | bytes 1474568 | tf_op jit(solution)/shard_map/ppermute | solution.py:14
  83.0 22.3 %all-to-all-start.2 = ((bf16[4,2,80,384]{3,2,1,0:T(8,128)(2,1)}), bf16[4,2,80,384]{3,2,1,0:T(8,128)(2,1)S(1)}, u32[]{:S(2)}, u32[]{:S(2)}) async-start(bf16[4,2,80,384]{3,2,1,0:T(8,128)(2,1)} %bitcast.79), calls=%async_computation.2 | async-start | bytes 983040 | tf_op jit(solution)/shard_map/all_to_all | solution.py:72
  105.7 49.9 %copy-start.1 = (f32[2,12,384]{2,0,1:T(2,128)S(1)}, f32[2,12,384]{2,0,1:T(2,128)}, u32[]{:S(2)}) copy-start(f32[2,12,384]{2,0,1:T(2,128)} %param.7) | copy-start | bytes 110596
  106.7 13.9 %all-to-all-start.3 = ((bf16[16,2,12,384]{3,1,2,0:T(2,128)(2,1)}), bf16[16,2,12,384]{3,1,2,0:T(2,128)(2,1)S(1)}, u32[]{:S(2)}, u32[]{:S(2)}) async-start(bf16[16,2,12,384]{3,1,2,0:T(2,128)(2,1)} %bitcast.21), calls=%async_computation.3 | async-start | bytes 589824 | tf_op jit(solution)/shard_map/all_to_all | solution.py:81
  110.3 4.3 %collective-permute-start.4 = (bf16[2,40,384]{2,1,0:T(8,128)(2,1)S(1)}, bf16[2,40,384]{2,1,0:T(8,128)(2,1)S(1)}, u32[]{:S(2)}, u32[]{:S(2)}) collective-permute-start(bf16[2,40,384]{2,1,0:T(8,128)(2,1)S(1)} %fusion.2), channel_id=1, source_target_pairs={{0,1},{1,0},{2,3},{3,2},{4,5},{5,4},{6,7},{7,6},{8,9},{9,8},{10,11... | collective-permute-start | bytes 184328 | tf_op jit(solution)/shard_map/ppermute | solution.py:14
  121.5 21.8 %all-to-all-start.4 = ((bf16[4,12,384]{2,1,0:T(8,128)(2,1)}), bf16[4,12,384]{2,1,0:T(8,128)(2,1)S(1)}, u32[]{:S(2)}, u32[]{:S(2)}) async-start(bf16[4,12,384]{2,1,0:T(8,128)(2,1)} %bitcast.28), calls=%async_computation.4 | async-start | bytes 98304 | tf_op jit(solution)/shard_map/all_to_all | solution.py:89
  131.2 19.2 %collective-permute-start.5 = (bf16[2,40,384]{2,1,0:T(8,128)(2,1)S(1)}, bf16[2,40,384]{2,1,0:T(8,128)(2,1)S(1)}, u32[]{:S(2)}, u32[]{:S(2)}) collective-permute-start(bf16[2,40,384]{2,1,0:T(8,128)(2,1)S(1)} %fusion.3), channel_id=1, source_target_pairs={{0,8},{8,0},{1,9},{9,1},{2,10},{10,2},{3,11},{11,3},{4,12},{12,4},... | collective-permute-start | bytes 184328 | tf_op jit(solution)/shard_map/ppermute | solution.py:14
  144.0 11.4 %all-to-all-start.5 = ((bf16[8,12,384]{2,1,0:T(8,128)(2,1)}), bf16[8,12,384]{2,1,0:T(8,128)(2,1)S(1)}, u32[]{:S(2)}, u32[]{:S(2)}) async-start(bf16[8,12,384]{2,1,0:T(8,128)(2,1)} %broadcast_in_dim.14), calls=%async_computation.5 | async-start | bytes 196608 | tf_op jit(solution)/shard_map/all_to_all | solution.py:29

commit v2 on v1

v2 whole, which is shorter than its diff:
```python
import jax
import jax.numpy as jnp
from jax import lax
from jax.sharding import Mesh, PartitionSpec as P

BS = 128
LATE = True
AXES = ("y", "g", "q", "zh", "x", "k")
SIZES = (4, 2, 4, 2, 4, 2)
ROW = ("y", "g", "q")
COL = ("zh", "x", "k")


def swapped(x, axis):
    return lax.ppermute(x, axis, [(0, 1), (1, 0)])


def to_columns():
    route = []
    for row in range(32):
        for col in range(16):
            zh, x, k = col // 8, (col // 2) % 4, col % 2
            target_row = ((row % 2) * 2 + zh) * 8 + k * 4 + x
            route.append((row * 16 + col, target_row * 16 + row // 2))
    return route


def gathered(x, axis):
    n = lax.axis_size(axis)
    return lax.all_to_all(jnp.broadcast_to(x[None], (n,) + x.shape), axis, 0, 0)


def ordered(mine, other, index):
    first = jnp.where(index == 0, mine, other)
    second = jnp.where(index == 0, other, mine)
    return jnp.stack([first, second])


def masked_pair(lower_panel, structure, k):
    rows = lower_panel.shape[0]
    flat = lower_panel.reshape(rows, 768)
    pair = ordered(flat, swapped(flat, "k"), k)
    start = (lax.axis_index(ROW) * 16 + lax.axis_index(COL) - k) * rows
    block = start // BS
    here = lax.dynamic_slice_in_dim(structure, block, 1, 0)
    after_it = lax.dynamic_slice_in_dim(structure, jnp.minimum(block + 1, structure.shape[0] - 1), 1, 0)
    row = start + lax.broadcasted_iota(jnp.int32, (2 * rows, 1), 0)
    keep = jnp.where(row < (block + 1) * BS, here, after_it).astype(jnp.bfloat16)
    keep = jnp.repeat(keep, 384, axis=1).reshape(2, rows, 768)
    return pair * keep


def added(parts):
    return jnp.sum(parts.astype(jnp.float32), axis=0)


def after(x, first):
    return lax.optimization_barrier((x, first))[0]


def turned(x, axis, d):
    n = lax.axis_size(axis)
    return lax.ppermute(x, axis, [(i, (i + d) % n) for i in range(n)])


def ring_of_four(x, axis):
    half = x.shape[0] // 2
    up, down = turned(x, axis, 1), turned(x, axis, 3)
    across = jnp.concatenate([turned(up[:half], axis, 1), turned(down[half:], axis, 3)])
    i = lax.axis_index(axis)
    by_distance = jnp.stack([x, up, across, down])
    order = [lax.dynamic_index_in_dim(by_distance, (i - j) % 4, 0, keepdims=False) for j in range(4)]
    return jnp.concatenate(order)


def piece(chunks, i):
    return lax.dynamic_index_in_dim(chunks, i, 1, keepdims=False)


def in_order(by_distance, x):
    return jnp.stack([lax.dynamic_index_in_dim(by_distance, (x - j) % 4, 1, keepdims=False) for j in range(4)], axis=1)


def panel(x, p):
    return x[..., p * 384 : (p + 1) * 384]


def shards(inverse_block, lower_panel, structure, diag_inverse):
    f32, bf16 = jnp.float32, jnp.bfloat16
    k = lax.axis_index("k")
    zh = lax.axis_index("zh")
    pair = masked_pair(lower_panel, structure, k)
    own_rows = jnp.where(k == 0, panel(pair, 0), panel(pair, 1))
    moved = lax.ppermute(pair, AXES, to_columns())
    quarter = lax.all_gather(moved.reshape(80, 768), "q", tiled=True)
    own_rows = after(own_rows, quarter)
    far_rows = swapped(own_rows, "zh")
    near_rows = ordered(own_rows, far_rows, zh)
    columns = ring_of_four(quarter, "y")
    by_distance = [near_rows] + [turned(near_rows, "x", d) for d in (1, 3, 2)]
    by_distance = jnp.stack([by_distance[j] for j in (0, 1, 3, 2)], axis=1)
    product = jnp.dot(inverse_block, columns, preferred_element_type=f32)
    products = [panel(product, p) for p in range(2)]

    mine = jnp.where(k == 0, products[0], products[1])
    sent = jnp.where(k == 0, products[1], products[0]).astype(bf16)
    summed = (mine + swapped(sent, "k").astype(f32)).astype(bf16)

    x = lax.axis_index("x")
    chunks = summed.reshape(2, 4, 80, 384)
    all_rows = in_order(by_distance, x).reshape(640, 384)
    schur = lax.dot_general(
        all_rows, summed, (((0,), (0,)), ((), ())), preferred_element_type=f32
    ).astype(bf16)
    by_yq = schur.reshape(4, 2, 4, 12, 384).transpose(0, 2, 1, 3, 4)
    by_yq = added(lax.all_to_all(by_yq.reshape(16, 2, 12, 384), ("y", "q"), 0, 0)).astype(bf16)

    if LATE:
        chunks = after(chunks, schur)
    parts = [piece(chunks, x)] + [turned(piece(chunks, (x + d) % 4), "x", d) for d in (1, 3, 2)]
    parts, _ = lax.optimization_barrier((parts, by_yq))
    near = added(jnp.stack(parts))
    near = near.astype(bf16).reshape(2, 2, 40, 384)

    kept = jnp.where(k == 0, near[:, 0], near[:, 1])
    other = swapped(jnp.where(k == 0, near[:, 1], near[:, 0]), "k")
    halves = jnp.stack([jnp.where(k == 0, kept, other), jnp.where(k == 0, other, kept)], axis=1)
    halves = after(halves, by_yq)
    by_z = jnp.broadcast_to(by_yq[:, None], (2, 2, 12, 384)).reshape(4, 12, 384)
    by_z = added(lax.all_to_all(by_z, ("g", "zh"), 0, 0)).astype(bf16)
    far_half = swapped(jnp.where(zh == 0, halves[1], halves[0]), "zh").astype(f32)
    own_half = jnp.where(zh == 0, halves[0], halves[1]).astype(f32)
    inverse_panel = (-(own_half + far_half)).astype(bf16).transpose(1, 0, 2)

    total = jnp.sum(gathered(by_z, ("x", "k")).reshape(4, 2, 12, 384).astype(f32), axis=0)
    return inverse_panel, diag_inverse + total


def solution(mesh):
    fine = Mesh(mesh.devices.reshape(SIZES), AXES)
    return jax.shard_map(
        shards,
        mesh=fine,
        in_specs=(P(ROW, COL), P(AXES, None, None), P(), P(None, ROW, None)),
        out_specs=(P(AXES, None, None), P(None, ROW, None)),
        check_vma=False,
    )
```

time: 157 us -> 151 us (0.962)
  waiting for transfers between devices: 43 us -> 14 us
  blocking collectives: 0 us -> 17.4 us
  starting transfers between devices: 99.3 us -> 106 us
  matrix products: 4.26 us -> 1.91 us
    ppermute x0 -> x10, starting transfers between devices: none -> 34.3 us  [turned(): return lax.ppermute(x, axis, [(i, (i + d) % n) for i in range(n)])]
    all_gather x0 -> x1, blocking collectives: none -> 17.4 us  [shards(): quarter = lax.all_gather(moved.reshape(80, 768), 'q', tiled=True)]
    all_to_all x3 -> x1, waiting for transfers between devices: 19.2 us -> 4.29 us  [gathered(): return lax.all_to_all(jnp.broadcast_to(x[None], (n,) + x.shape), axis, 0, 0)]
    all_to_all x1 -> x0, starting transfers between devices: 13.7 us -> none  [shards(): near = added(lax.all_to_all(chunks, 'x', 0, 0))]
    all_to_all x3 -> x1, starting transfers between devices: 18 us -> 4.83 us  [gathered(): return lax.all_to_all(jnp.broadcast_to(x[None], (n,) + x.shape), axis, 0, 0)]
    all_to_all x1 -> x0, waiting for transfers between devices: 8.51 us -> none  [shards(): near = added(lax.all_to_all(chunks, 'x', 0, 0))]
    ppermute x5, waiting for transfers between devices: 4.91 us -> 0.02 us  [swapped(): return lax.ppermute(x, axis, [(0, 1), (1, 0)])]
    all_to_all x1, waiting for transfers between devices: 5.96 us -> 1.69 us  [shards(): lax.all_to_all(by_yq.reshape(16, 2, 12, 384), ('y', 'q'), 0, 0)]
  transfers between devices with their start and end apart: 12 -> 19, of which waited for: 9 -> 4; matrix products, arithmetic and copies ran while one was open for 1% -> 5% of each run, Pallas kernels for 0% -> 0%
where the time goes in v2:
time: 151 us
  starting transfers between devices  106 us (70%)
  blocking collectives  17.4 us (12%)
  waiting for transfers between devices  14 us (9%)
  local copies, waits for them, and re-layouts  7.79 us (5%)
  other arithmetic  2.49 us (2%)
  matrix products  1.91 us (1%)
    ppermute x5, starting transfers between devices, swapped(): return lax.ppermute(x, axis, [(0, 1), (1, 0)])  52 us
    ppermute x10, starting transfers between devices, turned(): return lax.ppermute(x, axis, [(i, (i + d) % n) for i in range(n)])  34.3 us
    all_gather x1, blocking collectives, shards(): quarter = lax.all_gather(moved.reshape(80, 768), 'q', tiled=True)  17.4 us
    all_to_all x1, starting transfers between devices, shards(): by_z = added(lax.all_to_all(by_z, ('g', 'zh'), 0, 0)).astype(bf16)  6.93 us
    ppermute x1, waiting for transfers between devices, shards(): moved = lax.ppermute(pair, AXES, to_columns())  5.32 us
    all_to_all x1, starting transfers between devices, gathered(): return lax.all_to_all(jnp.broadcast_to(x[None], (n,) + x.shape), axis, 0, 0)  4.83 us
    all_to_all x1, waiting for transfers between devices, gathered(): return lax.all_to_all(jnp.broadcast_to(x[None], (n,) + x.shape), axis, 0, 0)  4.29 us
    all_to_all x1, starting transfers between devices, shards(): lax.all_to_all(by_yq.reshape(16, 2, 12, 384), ('y', 'q'), 0, 0)  4.15 us
  transfers between devices with their start and end apart: 19, of which 4 were waited for; matrix products, arithmetic and copies ran while one was open for 5% of the time, Pallas kernels for 0%

profile of v2, /device:TPU:1, one launch (start us, length us, event | category | flops | bytes accessed | tf_op | source)
XLA Modules:
  0.0 150.6 jit_solution(8557232972538343638)
XLA Ops:
  0.6 1.0 copy.95
  1.6 8.8 %collective-permute-start = (bf16[40,768]{1,0:T(8,128)(2,1)S(1)}, bf16[40,768]{1,0:T(8,128)(2,1)S(1)}, u32[]{:S(2)}, u32[]{:S(2)}) collective-permute-start(bf16[40,768]{1,0:T(8,128)(2,1)S(1)} %bitcast.114), channel_id=1, source_target_pairs={{0,1},{1,0},{2,3},{3,2},{4,5},{5,4},{6,7},{7,6},{8,9},{9,8},{10,11... | collective-permute-start | bytes 184328 | tf_op jit(solution)/shard_map/ppermute | solution.py:15
  10.5 1.0 fusion.17
  11.9 3.3 %collective-permute-start.1 = (bf16[2,40,768]{2,1,0:T(8,128)(2,1)S(1)}, bf16[2,40,768]{2,1,0:T(8,128)(2,1)S(1)}, u32[]{:S(2)}, u32[]{:S(2)}) collective-permute-start(bf16[2,40,768]{2,1,0:T(8,128)(2,1)S(1)} %maximum_multiply_fusion), channel_id=1, source_target_pairs={{0,0},{1,64},{2,16},{3,80},{4,32},{5,96},{6,48},{7,112},{8,128},{9... | collective-permute-start | bytes 368648 | tf_op jit(solution)/shard_map/ppermute | solution.py:94
  15.2 5.3 %collective-permute-done.1 = bf16[2,40,768]{2,1,0:T(8,128)(2,1)S(1)} collective-permute-done((bf16[2,40,768]{2,1,0:T(8,128)(2,1)S(1)}, bf16[2,40,768]{2,1,0:T(8,128)(2,1)S(1)}, u32[]{:S(2)}, u32[]{:S(2)}) %collective-permute-start.1) | collective-permute-done | bytes 122912 | tf_op jit(solution)/shard_map/ppermute | solution.py:94
  20.5 17.4 %all_gather.3 = bf16[320,768]{1,0:T(8,128)(2,1)S(1)} all-gather(bf16[80,768]{1,0:T(8,128)(2,1)S(1)} %bitcast.116), channel_id=1, replica_groups=mesh['y'=4,'g'=2,'q'=4,'zh'=2,'x'=4,'k'=2] {'q'}, dimensions={0}, use_global_device_ids=true | all-gather | bytes 614400 | tf_op jit(solution)/shard_map/all_gather | solution.py:95
  38.0 6.1 %collective-permute-start.2 = (bf16[320,768]{1,0:T(8,128)(2,1)S(1)}, bf16[320,768]{1,0:T(8,128)(2,1)S(1)}, u32[]{:S(2)}, u32[]{:S(2)}) collective-permute-start(bf16[320,768]{1,0:T(8,128)(2,1)S(1)} %all_gather.3), channel_id=1, source_target_pairs={{0,128},{128,256},{256,384},{384,0},{1,129},{129,257},{257,385},{3... | collective-permute-start | bytes 1474568 | tf_op jit(solution)/shard_map/ppermute | solution.py:63
  44.1 4.3 %collective-permute-start.4 = (bf16[320,768]{1,0:T(8,128)(2,1)S(1)}, bf16[320,768]{1,0:T(8,128)(2,1)S(1)}, u32[]{:S(2)}, u32[]{:S(2)}) collective-permute-start(bf16[320,768]{1,0:T(8,128)(2,1)S(1)} %all_gather.3), channel_id=1, source_target_pairs={{0,384},{128,0},{256,128},{384,256},{1,385},{129,1},{257,129},{385... | collective-permute-start | bytes 1474568 | tf_op jit(solution)/shard_map/ppermute | solution.py:63
  48.4 20.2 %collective-permute-start.7 = (bf16[2,40,384]{2,1,0:T(8,128)(2,1)S(1)}, bf16[2,40,384]{2,1,0:T(8,128)(2,1)S(1)}, u32[]{:S(2)}, u32[]{:S(2)}) collective-permute-start(bf16[2,40,384]{2,1,0:T(8,128)(2,1)S(1)} %slice_select_fusion), channel_id=1, source_target_pairs={{0,8},{8,0},{1,9},{9,1},{2,10},{10,2},{3,11},{11,3},{4,12},{12,4},... | collective-permute-start | bytes 184328 | tf_op jit(solution)/shard_map/ppermute | solution.py:15
  68.8 1.9 %collective-permute-start.3 = (bf16[160,768]{1,0:T(8,128)(2,1)S(1)}, bf16[160,768]{1,0:T(8,128)(2,1)S(1)}, u32[]{:S(2)}, u32[]{:S(2)}) collective-permute-start(bf16[160,768]{1,0:T(8,128)(2,1)S(1)} %slice.44), channel_id=1, source_target_pairs={{0,128},{128,256},{256,384},{384,0},{1,129},{129,257},{257,385},{3... | collective-permute-start | bytes 737288 | tf_op jit(solution)/shard_map/ppermute | solution.py:63
  70.7 4.6 %collective-permute-start.5 = (bf16[160,768]{1,0:T(8,128)(2,1)S(1)}, bf16[160,768]{1,0:T(8,128)(2,1)S(1)}, u32[]{:S(2)}, u32[]{:S(2)}) collective-permute-start(bf16[160,768]{1,0:T(8,128)(2,1)S(1)} %slice.45), channel_id=1, source_target_pairs={{0,384},{128,0},{256,128},{384,256},{1,385},{129,1},{257,129},{385... | collective-permute-start | bytes 737288 | tf_op jit(solution)/shard_map/ppermute | solution.py:63
  75.4 1.9 %collective-permute-start.8 = (bf16[2,2,40,384]{3,2,1,0:T(8,128)(2,1)S(1)}, bf16[2,2,40,384]{3,2,1,0:T(8,128)(2,1)S(1)}, u32[]{:S(2)}, u32[]{:S(2)}) collective-permute-start(bf16[2,2,40,384]{3,2,1,0:T(8,128)(2,1)S(1)} %get-tuple-element.45), channel_id=1, source_target_pairs={{0,2},{2,4},{4,6},{6,0},{1,3},{3,5},{5,7},{7,1},{8,10},{10,12},{12... | collective-permute-start | bytes 368648 | tf_op jit(solution)/shard_map/ppermute | solution.py:63
  77.3 1.9 %collective-permute-start.9 = (bf16[2,2,40,384]{3,2,1,0:T(8,128)(2,1)S(1)}, bf16[2,2,40,384]{3,2,1,0:T(8,128)(2,1)}, u32[]{:S(2)}, u32[]{:S(2)}) collective-permute-start(bf16[2,2,40,384]{3,2,1,0:T(8,128)(2,1)S(1)} %get-tuple-element.45), channel_id=1, source_target_pairs={{0,4},{2,6},{4,0},{6,2},{1,5},{3,7},{5,1},{7,3},{8,12},{10,14},{12... | collective-permute-start | bytes 368648 | tf_op jit(solution)/shard_map/ppermute | solution.py:63
  79.2 4.6 %collective-permute-start.10 = (bf16[2,2,40,384]{3,2,1,0:T(8,128)(2,1)S(1)}, bf16[2,2,40,384]{3,2,1,0:T(8,128)(2,1)}, u32[]{:S(2)}, u32[]{:S(2)}) collective-permute-start(bf16[2,2,40,384]{3,2,1,0:T(8,128)(2,1)S(1)} %get-tuple-element.45), channel_id=1, source_target_pairs={{0,6},{2,0},{4,2},{6,4},{1,7},{3,1},{5,3},{7,5},{8,14},{10,8},{12,... | collective-permute-start | bytes 368648 | tf_op jit(solution)/shard_map/ppermute | solution.py:63
  84.3 1.4 fusion.8
  85.8 1.3 copy-done.1
  87.1 6.9 %collective-permute-start.6 = (bf16[640,384]{1,0:T(8,128)(2,1)S(1)}, bf16[640,384]{1,0:T(8,128)(2,1)S(1)}, u32[]{:S(2)}, u32[]{:S(2)}) collective-permute-start(bf16[640,384]{1,0:T(8,128)(2,1)S(1)} %select_convert_fusion), channel_id=1, source_target_pairs={{0,1},{1,0},{2,3},{3,2},{4,5},{5,4},{6,7},{7,6},{8,9},{9,8},{10,11... | collective-permute-start | bytes 1474568 | tf_op jit(solution)/shard_map/ppermute | solution.py:15
  94.1 1.2 pad_maximum_fusion.1
  96.5 1.0 copy.77
  97.5 4.1 %all-to-all-start = ((bf16[16,2,12,384]{3,1,2,0:T(2,128)(2,1)}), bf16[16,2,12,384]{3,1,2,0:T(2,128)(2,1)S(1)}, u32[]{:S(2)}, u32[]{:S(2)}) async-start(bf16[16,2,12,384]{3,1,2,0:T(2,128)(2,1)} %bitcast.28), calls=%async_computation | async-start | bytes 589824 | tf_op jit(solution)/shard_map/all_to_all | solution.py:116
  101.8 1.9 %collective-permute-start.11 = (bf16[2,80,384]{2,1,0:T(8,128)(2,1)S(1)}, bf16[2,80,384]{2,1,0:T(8,128)(2,1)S(1)}, u32[]{:S(2)}, u32[]{:S(2)}) collective-permute-start(bf16[2,80,384]{2,1,0:T(8,128)(2,1)S(1)} %get-tuple-element.36), channel_id=1, source_target_pairs={{0,2},{2,4},{4,6},{6,0},{1,3},{3,5},{5,7},{7,1},{8,10},{10,12},{12... | collective-permute-start | bytes 368648 | tf_op jit(solution)/shard_map/ppermute | solution.py:63
  103.7 4.6 %collective-permute-start.12 = (bf16[2,80,384]{2,1,0:T(8,128)(2,1)S(1)}, bf16[2,80,384]{2,1,0:T(8,128)(2,1)S(1)}, u32[]{:S(2)}, u32[]{:S(2)}) collective-permute-start(bf16[2,80,384]{2,1,0:T(8,128)(2,1)S(1)} %get-tuple-element.35), channel_id=1, source_target_pairs={{0,6},{2,0},{4,2},{6,4},{1,7},{3,1},{5,3},{7,5},{8,14},{10,8},{12,... | collective-permute-start | bytes 368648 | tf_op jit(solution)/shard_map/ppermute | solution.py:63
  108.3 2.5 %collective-permute-start.13 = (bf16[2,80,384]{2,1,0:T(8,128)(2,1)S(1)}, bf16[2,80,384]{2,1,0:T(8,128)(2,1)S(1)}, u32[]{:S(2)}, u32[]{:S(2)}) collective-permute-start(bf16[2,80,384]{2,1,0:T(8,128)(2,1)S(1)} %get-tuple-element.34), channel_id=1, source_target_pairs={{0,4},{2,6},{4,0},{6,2},{1,5},{3,7},{5,1},{7,3},{8,12},{10,14},{12... | collective-permute-start | bytes 368648 | tf_op jit(solution)/shard_map/ppermute | solution.py:63
  110.8 1.7 %all-to-all-done = bf16[16,2,12,384]{3,1,2,0:T(2,128)(2,1)S(1)} async-done(((bf16[16,2,12,384]{3,1,2,0:T(2,128)(2,1)}), bf16[16,2,12,384]{3,1,2,0:T(2,128)(2,1)S(1)}, u32[]{:S(2)}, u32[]{:S(2)}) %all-to-all-start) | async-done | bytes 294944 | tf_op jit(solution)/shard_map/all_to_all | solution.py:116
  112.8 2.6 %collective-permute-done.13 = bf16[2,80,384]{2,1,0:T(8,128)(2,1)S(1)} collective-permute-done((bf16[2,80,384]{2,1,0:T(8,128)(2,1)S(1)}, bf16[2,80,384]{2,1,0:T(8,128)(2,1)S(1)}, u32[]{:S(2)}, u32[]{:S(2)}) %collective-permute-start.13) | collective-permute-done | bytes 122912 | tf_op jit(solution)/shard_map/ppermute | solution.py:63
  115.5 4.0 %collective-permute-start.14 = (bf16[2,40,384]{2,1,0:T(8,128)(2,1)S(1)}, bf16[2,40,384]{2,1,0:T(8,128)(2,1)S(1)}, u32[]{:S(2)}, u32[]{:S(2)}) collective-permute-start(bf16[2,40,384]{2,1,0:T(8,128)(2,1)S(1)} %select_bitcast_fusion), channel_id=1, source_target_pairs={{0,1},{1,0},{2,3},{3,2},{4,5},{5,4},{6,7},{7,6},{8,9},{9,8},{10,11... | collective-permute-start | bytes 184328 | tf_op jit(solution)/shard_map/ppermute | solution.py:15
  120.1 6.9 %all-to-all-start.1 = ((bf16[4,12,384]{2,1,0:T(8,128)(2,1)}), bf16[4,12,384]{2,1,0:T(8,128)(2,1)S(1)}, u32[]{:S(2)}, u32[]{:S(2)}) async-start(bf16[4,12,384]{2,1,0:T(8,128)(2,1)} %bitcast.40), calls=%async_computation.1 | async-start | bytes 98304 | tf_op jit(solution)/shard_map/all_to_all | solution.py:130
  127.1 12.1 %collective-permute-start.15 = (bf16[2,40,384]{2,1,0:T(8,128)(2,1)S(1)}, bf16[2,40,384]{2,1,0:T(8,128)(2,1)S(1)}, u32[]{:S(2)}, u32[]{:S(2)}) collective-permute-start(bf16[2,40,384]{2,1,0:T(8,128)(2,1)S(1)} %fusion.13), channel_id=1, source_target_pairs={{0,8},{8,0},{1,9},{9,1},{2,10},{10,2},{3,11},{11,3},{4,12},{12,4},... | collective-permute-start | bytes 184328 | tf_op jit(solution)/shard_map/ppermute | solution.py:15
  139.3 0.6 broadcast_in_dim.50
  139.9 4.8 %all-to-all-start.2 = ((bf16[8,12,384]{2,1,0:T(8,128)(2,1)}), bf16[8,12,384]{2,1,0:T(8,128)(2,1)S(1)}, u32[]{:S(2)}, u32[]{:S(2)}) async-start(bf16[8,12,384]{2,1,0:T(8,128)(2,1)} %broadcast_in_dim.50), calls=%async_computation.2 | async-start | bytes 196608 | tf_op jit(solution)/shard_map/all_to_all | solution.py:30
  144.8 0.7 copy.89
  145.4 4.3 %all-to-all-done.2 = bf16[8,12,384]{2,1,0:T(8,128)(2,1)S(1)} async-done(((bf16[8,12,384]{2,1,0:T(8,128)(2,1)}), bf16[8,12,384]{2,1,0:T(8,128)(2,1)S(1)}, u32[]{:S(2)}, u32[]{:S(2)}) %all-to-all-start.2) | async-done | bytes 73760 | tf_op jit(solution)/shard_map/all_to_all | solution.py:30
  (58 shorter events, 4.1 us)
Async XLA Ops:
  0.6 83.7 %copy-start = (bf16[640,1280]{1,0:T(8,128)(2,1)S(1)}, bf16[640,1280]{1,0:T(8,128)(2,1)}, u32[]{:S(2)}) copy-start(bf16[640,1280]{1,0:T(8,128)(2,1)} %param.4) | copy-start | bytes 4915204
  1.6 10.2 %collective-permute-start = (bf16[40,768]{1,0:T(8,128)(2,1)S(1)}, bf16[40,768]{1,0:T(8,128)(2,1)S(1)}, u32[]{:S(2)}, u32[]{:S(2)}) collective-permute-start(bf16[40,768]{1,0:T(8,128)(2,1)S(1)} %bitcast.114), channel_id=1, source_target_pairs={{0,1},{1,0},{2,3},{3,2},{4,5},{5,4},{6,7},{7,6},{8,9},{9,8},{10,11... | collective-permute-start | bytes 184328 | tf_op jit(solution)/shard_map/ppermute | solution.py:15
  11.9 8.7 %collective-permute-start.1 = (bf16[2,40,768]{2,1,0:T(8,128)(2,1)S(1)}, bf16[2,40,768]{2,1,0:T(8,128)(2,1)S(1)}, u32[]{:S(2)}, u32[]{:S(2)}) collective-permute-start(bf16[2,40,768]{2,1,0:T(8,128)(2,1)S(1)} %maximum_multiply_fusion), channel_id=1, source_target_pairs={{0,0},{1,64},{2,16},{3,80},{4,32},{5,96},{6,48},{7,112},{8,128},{9... | collective-permute-start | bytes 368648 | tf_op jit(solution)/shard_map/ppermute | solution.py:94
  38.0 30.8 %collective-permute-start.2 = (bf16[320,768]{1,0:T(8,128)(2,1)S(1)}, bf16[320,768]{1,0:T(8,128)(2,1)S(1)}, u32[]{:S(2)}, u32[]{:S(2)}) collective-permute-start(bf16[320,768]{1,0:T(8,128)(2,1)S(1)} %all_gather.3), channel_id=1, source_target_pairs={{0,128},{128,256},{256,384},{384,0},{1,129},{129,257},{257,385},{3... | collective-permute-start | bytes 1474568 | tf_op jit(solution)/shard_map/ppermute | solution.py:63
  44.1 26.6 %collective-permute-start.4 = (bf16[320,768]{1,0:T(8,128)(2,1)S(1)}, bf16[320,768]{1,0:T(8,128)(2,1)S(1)}, u32[]{:S(2)}, u32[]{:S(2)}) collective-permute-start(bf16[320,768]{1,0:T(8,128)(2,1)S(1)} %all_gather.3), channel_id=1, source_target_pairs={{0,384},{128,0},{256,128},{384,256},{1,385},{129,1},{257,129},{385... | collective-permute-start | bytes 1474568 | tf_op jit(solution)/shard_map/ppermute | solution.py:63
  48.4 26.9 %collective-permute-start.7 = (bf16[2,40,384]{2,1,0:T(8,128)(2,1)S(1)}, bf16[2,40,384]{2,1,0:T(8,128)(2,1)S(1)}, u32[]{:S(2)}, u32[]{:S(2)}) collective-permute-start(bf16[2,40,384]{2,1,0:T(8,128)(2,1)S(1)} %slice_select_fusion), channel_id=1, source_target_pairs={{0,8},{8,0},{1,9},{9,1},{2,10},{10,2},{3,11},{11,3},{4,12},{12,4},... | collective-permute-start | bytes 184328 | tf_op jit(solution)/shard_map/ppermute | solution.py:15
  68.8 15.1 %collective-permute-start.3 = (bf16[160,768]{1,0:T(8,128)(2,1)S(1)}, bf16[160,768]{1,0:T(8,128)(2,1)S(1)}, u32[]{:S(2)}, u32[]{:S(2)}) collective-permute-start(bf16[160,768]{1,0:T(8,128)(2,1)S(1)} %slice.44), channel_id=1, source_target_pairs={{0,128},{128,256},{256,384},{384,0},{1,129},{129,257},{257,385},{3... | collective-permute-start | bytes 737288 | tf_op jit(solution)/shard_map/ppermute | solution.py:63
  70.7 13.1 %collective-permute-start.5 = (bf16[160,768]{1,0:T(8,128)(2,1)S(1)}, bf16[160,768]{1,0:T(8,128)(2,1)S(1)}, u32[]{:S(2)}, u32[]{:S(2)}) collective-permute-start(bf16[160,768]{1,0:T(8,128)(2,1)S(1)} %slice.45), channel_id=1, source_target_pairs={{0,384},{128,0},{256,128},{384,256},{1,385},{129,1},{257,129},{385... | collective-permute-start | bytes 737288 | tf_op jit(solution)/shard_map/ppermute | solution.py:63
  75.4 18.7 %collective-permute-start.8 = (bf16[2,2,40,384]{3,2,1,0:T(8,128)(2,1)S(1)}, bf16[2,2,40,384]{3,2,1,0:T(8,128)(2,1)S(1)}, u32[]{:S(2)}, u32[]{:S(2)}) collective-permute-start(bf16[2,2,40,384]{3,2,1,0:T(8,128)(2,1)S(1)} %get-tuple-element.45), channel_id=1, source_target_pairs={{0,2},{2,4},{4,6},{6,0},{1,3},{3,5},{5,7},{7,1},{8,10},{10,12},{12... | collective-permute-start | bytes 368648 | tf_op jit(solution)/shard_map/ppermute | solution.py:63
  77.3 16.8 %collective-permute-start.9 = (bf16[2,2,40,384]{3,2,1,0:T(8,128)(2,1)S(1)}, bf16[2,2,40,384]{3,2,1,0:T(8,128)(2,1)}, u32[]{:S(2)}, u32[]{:S(2)}) collective-permute-start(bf16[2,2,40,384]{3,2,1,0:T(8,128)(2,1)S(1)} %get-tuple-element.45), channel_id=1, source_target_pairs={{0,4},{2,6},{4,0},{6,2},{1,5},{3,7},{5,1},{7,3},{8,12},{10,14},{12... | collective-permute-start | bytes 368648 | tf_op jit(solution)/shard_map/ppermute | solution.py:63
  79.2 14.9 %collective-permute-start.10 = (bf16[2,2,40,384]{3,2,1,0:T(8,128)(2,1)S(1)}, bf16[2,2,40,384]{3,2,1,0:T(8,128)(2,1)}, u32[]{:S(2)}, u32[]{:S(2)}) collective-permute-start(bf16[2,2,40,384]{3,2,1,0:T(8,128)(2,1)S(1)} %get-tuple-element.45), channel_id=1, source_target_pairs={{0,6},{2,0},{4,2},{6,4},{1,7},{3,1},{5,3},{7,5},{8,14},{10,8},{12,... | collective-permute-start | bytes 368648 | tf_op jit(solution)/shard_map/ppermute | solution.py:63
  85.8 1.3 copy-start.1
  87.1 8.4 %collective-permute-start.6 = (bf16[640,384]{1,0:T(8,128)(2,1)S(1)}, bf16[640,384]{1,0:T(8,128)(2,1)S(1)}, u32[]{:S(2)}, u32[]{:S(2)}) collective-permute-start(bf16[640,384]{1,0:T(8,128)(2,1)S(1)} %select_convert_fusion), channel_id=1, source_target_pairs={{0,1},{1,0},{2,3},{3,2},{4,5},{5,4},{6,7},{7,6},{8,9},{9,8},{10,11... | collective-permute-start | bytes 1474568 | tf_op jit(solution)/shard_map/ppermute | solution.py:15
  94.1 1.7 %copy-start.2 = (f32[640,768]{1,0:T(8,128)S(1)}, f32[640,768]{1,0:T(8,128)}, u32[]{:S(2)}) copy-start(f32[640,768]{1,0:T(8,128)} %copy-done.1) | copy-start | bytes 5898244
  97.5 15.0 %all-to-all-start = ((bf16[16,2,12,384]{3,1,2,0:T(2,128)(2,1)}), bf16[16,2,12,384]{3,1,2,0:T(2,128)(2,1)S(1)}, u32[]{:S(2)}, u32[]{:S(2)}) async-start(bf16[16,2,12,384]{3,1,2,0:T(2,128)(2,1)} %bitcast.28), calls=%async_computation | async-start | bytes 589824 | tf_op jit(solution)/shard_map/all_to_all | solution.py:116
  101.8 48.1 %copy-start.3 = (f32[2,12,384]{2,0,1:T(2,128)S(1)}, f32[2,12,384]{2,0,1:T(2,128)}, u32[]{:S(2)}) copy-start(f32[2,12,384]{2,0,1:T(2,128)} %param.7) | copy-start | bytes 110596
  101.8 11.0 %collective-permute-start.11 = (bf16[2,80,384]{2,1,0:T(8,128)(2,1)S(1)}, bf16[2,80,384]{2,1,0:T(8,128)(2,1)S(1)}, u32[]{:S(2)}, u32[]{:S(2)}) collective-permute-start(bf16[2,80,384]{2,1,0:T(8,128)(2,1)S(1)} %get-tuple-element.36), channel_id=1, source_target_pairs={{0,2},{2,4},{4,6},{6,0},{1,3},{3,5},{5,7},{7,1},{8,10},{10,12},{12... | collective-permute-start | bytes 368648 | tf_op jit(solution)/shard_map/ppermute | solution.py:63
  103.7 9.1 %collective-permute-start.12 = (bf16[2,80,384]{2,1,0:T(8,128)(2,1)S(1)}, bf16[2,80,384]{2,1,0:T(8,128)(2,1)S(1)}, u32[]{:S(2)}, u32[]{:S(2)}) collective-permute-start(bf16[2,80,384]{2,1,0:T(8,128)(2,1)S(1)} %get-tuple-element.35), channel_id=1, source_target_pairs={{0,6},{2,0},{4,2},{6,4},{1,7},{3,1},{5,3},{7,5},{8,14},{10,8},{12,... | collective-permute-start | bytes 368648 | tf_op jit(solution)/shard_map/ppermute | solution.py:63
  108.3 7.1 %collective-permute-start.13 = (bf16[2,80,384]{2,1,0:T(8,128)(2,1)S(1)}, bf16[2,80,384]{2,1,0:T(8,128)(2,1)S(1)}, u32[]{:S(2)}, u32[]{:S(2)}) collective-permute-start(bf16[2,80,384]{2,1,0:T(8,128)(2,1)S(1)} %get-tuple-element.34), channel_id=1, source_target_pairs={{0,4},{2,6},{4,0},{6,2},{1,5},{3,7},{5,1},{7,3},{8,12},{10,14},{12... | collective-permute-start | bytes 368648 | tf_op jit(solution)/shard_map/ppermute | solution.py:63
  115.5 11.6 %collective-permute-start.14 = (bf16[2,40,384]{2,1,0:T(8,128)(2,1)S(1)}, bf16[2,40,384]{2,1,0:T(8,128)(2,1)S(1)}, u32[]{:S(2)}, u32[]{:S(2)}) collective-permute-start(bf16[2,40,384]{2,1,0:T(8,128)(2,1)S(1)} %select_bitcast_fusion), channel_id=1, source_target_pairs={{0,1},{1,0},{2,3},{3,2},{4,5},{5,4},{6,7},{7,6},{8,9},{9,8},{10,11... | collective-permute-start | bytes 184328 | tf_op jit(solution)/shard_map/ppermute | solution.py:15
  120.1 19.1 %all-to-all-start.1 = ((bf16[4,12,384]{2,1,0:T(8,128)(2,1)}), bf16[4,12,384]{2,1,0:T(8,128)(2,1)S(1)}, u32[]{:S(2)}, u32[]{:S(2)}) async-start(bf16[4,12,384]{2,1,0:T(8,128)(2,1)} %bitcast.40), calls=%async_computation.1 | async-start | bytes 98304 | tf_op jit(solution)/shard_map/all_to_all | solution.py:130
  127.1 17.6 %collective-permute-start.15 = (bf16[2,40,384]{2,1,0:T(8,128)(2,1)S(1)}, bf16[2,40,384]{2,1,0:T(8,128)(2,1)S(1)}, u32[]{:S(2)}, u32[]{:S(2)}) collective-permute-start(bf16[2,40,384]{2,1,0:T(8,128)(2,1)S(1)} %fusion.13), channel_id=1, source_target_pairs={{0,8},{8,0},{1,9},{9,1},{2,10},{10,2},{3,11},{11,3},{4,12},{12,4},... | collective-permute-start | bytes 184328 | tf_op jit(solution)/shard_map/ppermute | solution.py:15
  139.9 9.8 %all-to-all-start.2 = ((bf16[8,12,384]{2,1,0:T(8,128)(2,1)}), bf16[8,12,384]{2,1,0:T(8,128)(2,1)S(1)}, u32[]{:S(2)}, u32[]{:S(2)}) async-start(bf16[8,12,384]{2,1,0:T(8,128)(2,1)} %broadcast_in_dim.50), calls=%async_computation.2 | async-start | bytes 196608 | tf_op jit(solution)/shard_map/all_to_all | solution.py:30

commit v3 on v2

--- a/solution.py
+++ b/solution.py
@@ -4,16 +4,14 @@
 from jax.sharding import Mesh, PartitionSpec as P
 
 BS = 128
-LATE = True
+
 AXES = ("y", "g", "q", "zh", "x", "k")
 SIZES = (4, 2, 4, 2, 4, 2)
 ROW = ("y", "g", "q")
 COL = ("zh", "x", "k")
 
-
 def swapped(x, axis):
     return lax.ppermute(x, axis, [(0, 1), (1, 0)])
-
 
 def to_columns():
     route = []
@@ -24,17 +22,14 @@
             route.append((row * 16 + col, target_row * 16 + row // 2))
     return route
 
-
 def gathered(x, axis):
     n = lax.axis_size(axis)
     return lax.all_to_all(jnp.broadcast_to(x[None], (n,) + x.shape), axis, 0, 0)
-
 
 def ordered(mine, other, index):
     first = jnp.where(index == 0, mine, other)
     second = jnp.where(index == 0, other, mine)
     return jnp.stack([first, second])
-
 
 def masked_pair(lower_panel, structure, k):
     rows = lower_panel.shape[0]
@@ -49,19 +44,15 @@
     keep = jnp.repeat(keep, 384, axis=1).reshape(2, rows, 768)
     return pair * keep
 
-
 def added(parts):
     return jnp.sum(parts.astype(jnp.float32), axis=0)
-
 
 def after(x, first):
     return lax.optimization_barrier((x, first))[0]
 
-
 def turned(x, axis, d):
     n = lax.axis_size(axis)
     return lax.ppermute(x, axis, [(i, (i + d) % n) for i in range(n)])
-
 
 def ring_of_four(x, axis):
     half = x.shape[0] // 2
@@ -72,18 +63,14 @@
     order = [lax.dynamic_index_in_dim(by_distance, (i - j) % 4, 0, keepdims=False) for j in range(4)]
     return jnp.concatenate(order)
 
-
 def piece(chunks, i):
     return lax.dynamic_index_in_dim(chunks, i, 1, keepdims=False)
-
 
 def in_order(by_distance, x):
     return jnp.stack([lax.dynamic_index_in_dim(by_distance, (x - j) % 4, 1, keepdims=False) for j in range(4)], axis=1)
 
-
 def panel(x, p):
     return x[..., p * 384 : (p + 1) * 384]
-
 
 def shards(inverse_block, lower_panel, structure, diag_inverse):
     f32, bf16 = jnp.float32, jnp.bfloat16
@@ -92,19 +79,18 @@
     pair = masked_pair(lower_panel, structure, k)
     own_rows = jnp.where(k == 0, panel(pair, 0), panel(pair, 1))
     moved = lax.ppermute(pair, AXES, to_columns())
+    moved = jnp.where(k == 0, moved, jnp.concatenate([panel(moved, 1), panel(moved, 0)], axis=-1))
     quarter = lax.all_gather(moved.reshape(80, 768), "q", tiled=True)
-    own_rows = after(own_rows, quarter)
     far_rows = swapped(own_rows, "zh")
     near_rows = ordered(own_rows, far_rows, zh)
     columns = ring_of_four(quarter, "y")
+    own_columns, other_columns = panel(columns, 0), panel(columns, 1)
     by_distance = [near_rows] + [turned(near_rows, "x", d) for d in (1, 3, 2)]
     by_distance = jnp.stack([by_distance[j] for j in (0, 1, 3, 2)], axis=1)
-    product = jnp.dot(inverse_block, columns, preferred_element_type=f32)
-    products = [panel(product, p) for p in range(2)]
 
-    mine = jnp.where(k == 0, products[0], products[1])
-    sent = jnp.where(k == 0, products[1], products[0]).astype(bf16)
-    summed = (mine + swapped(sent, "k").astype(f32)).astype(bf16)
+    sent = jnp.dot(inverse_block, other_columns, preferred_element_type=f32).astype(bf16)
+    arrived = swapped(sent, "k")
+    summed = (jnp.dot(inverse_block, own_columns, preferred_element_type=f32) + arrived.astype(f32)).astype(bf16)
 
     x = lax.axis_index("x")
     chunks = summed.reshape(2, 4, 80, 384)
@@ -115,8 +101,7 @@
     by_yq = schur.reshape(4, 2, 4, 12, 384).transpose(0, 2, 1, 3, 4)
     by_yq = added(lax.all_to_all(by_yq.reshape(16, 2, 12, 384), ("y", "q"), 0, 0)).astype(bf16)
 
-    if LATE:
-        chunks = after(chunks, schur)
+    chunks = after(chunks, schur)
     parts = [piece(chunks, x)] + [turned(piece(chunks, (x + d) % 4), "x", d) for d in (1, 3, 2)]
     parts, _ = lax.optimization_barrier((parts, by_yq))
     near = added(jnp.stack(parts))
@@ -135,7 +120,6 @@
     total = jnp.sum(gathered(by_z, ("x", "k")).reshape(4, 2, 12, 384).astype(f32), axis=0)
     return inverse_panel, diag_inverse + total
 
-
 def solution(mesh):
     fine = Mesh(mesh.devices.reshape(SIZES), AXES)
     return jax.shard_map(

time: 151 us -> 151 us (level)
    ppermute x10, starting transfers between devices: 34.3 us -> 32.5 us  [turned(): return lax.ppermute(x, axis, [(i, (i + d) % n) for i in range(n)])]
    all_to_all x1, starting transfers between devices: 4.15 us -> 5.89 us  [shards(): lax.all_to_all(by_yq.reshape(16, 2, 12, 384), ('y', 'q'), 0, 0)]
    all_to_all x1, waiting for transfers between devices: 1.69 us -> 0.01 us  [shards(): lax.all_to_all(by_yq.reshape(16, 2, 12, 384), ('y', 'q'), 0, 0)]
  transfers between devices with their start and end apart: 19 -> 19, of which waited for: 4 -> 3; matrix products, arithmetic and copies ran while one was open for 5% -> 5% of each run, Pallas kernels for 0% -> 0%
where the time goes in v3:
time: 151 us; the launch traced here: 150 us
  starting transfers between devices  105 us (70%)
  blocking collectives  18.7 us (12%)
  waiting for transfers between devices  12.6 us (8%)
  local copies, waits for them, and re-layouts  7.11 us (5%)
  matrix products  2.47 us (2%)
  other arithmetic  2.39 us (2%)
    ppermute x5, starting transfers between devices, swapped(): return lax.ppermute(x, axis, [(0, 1), (1, 0)])  51 us
    ppermute x10, starting transfers between devices, turned(): return lax.ppermute(x, axis, [(i, (i + d) % n) for i in range(n)])  32.5 us
    all_gather x1, blocking collectives, shards(): quarter = lax.all_gather(moved.reshape(80, 768), 'q', tiled=True)  18.7 us
    all_to_all x1, starting transfers between devices, shards(): by_z = added(lax.all_to_all(by_z, ('g', 'zh'), 0, 0)).astype(bf16)  7.71 us
    all_to_all x1, starting transfers between devices, shards(): lax.all_to_all(by_yq.reshape(16, 2, 12, 384), ('y', 'q'), 0, 0)  5.89 us
    ppermute x1, waiting for transfers between devices, shards(): moved = lax.ppermute(pair, AXES, to_columns())  5.32 us
    all_to_all x1, starting transfers between devices, gathered(): return lax.all_to_all(jnp.broadcast_to(x[None], (n,) + x.shape), axis, 0, 0)  4.81 us
    all_to_all x1, waiting for transfers between devices, gathered(): return lax.all_to_all(jnp.broadcast_to(x[None], (n,) + x.shape), axis, 0, 0)  4.29 us
  transfers between devices with their start and end apart: 19, of which 3 were waited for; matrix products, arithmetic and copies ran while one was open for 5% of the time, Pallas kernels for 0%

profile of v3, /device:TPU:1, one launch (start us, length us, event | category | flops | bytes accessed | tf_op | source)
XLA Modules:
  0.0 149.8 jit_solution(1950226623689387528)
XLA Ops:
  0.6 1.0 copy.101
  1.6 8.8 %collective-permute-start = (bf16[40,768]{1,0:T(8,128)(2,1)S(1)}, bf16[40,768]{1,0:T(8,128)(2,1)S(1)}, u32[]{:S(2)}, u32[]{:S(2)}) collective-permute-start(bf16[40,768]{1,0:T(8,128)(2,1)S(1)} %bitcast.118), channel_id=1, source_target_pairs={{0,1},{1,0},{2,3},{3,2},{4,5},{5,4},{6,7},{7,6},{8,9},{9,8},{10,11... | collective-permute-start | bytes 184328 | tf_op jit(solution)/shard_map/ppermute | solution.py:14
  10.5 1.0 fusion.9
  11.9 3.3 %collective-permute-start.1 = (bf16[2,40,768]{2,1,0:T(8,128)(2,1)S(1)}, bf16[2,40,768]{2,1,0:T(8,128)(2,1)S(1)}, u32[]{:S(2)}, u32[]{:S(2)}) collective-permute-start(bf16[2,40,768]{2,1,0:T(8,128)(2,1)S(1)} %maximum_multiply_fusion), channel_id=1, source_target_pairs={{0,0},{1,64},{2,16},{3,80},{4,32},{5,96},{6,48},{7,112},{8,128},{9... | collective-permute-start | bytes 368648 | tf_op jit(solution)/shard_map/ppermute | solution.py:81
  15.2 5.3 %collective-permute-done.1 = bf16[2,40,768]{2,1,0:T(8,128)(2,1)S(1)} collective-permute-done((bf16[2,40,768]{2,1,0:T(8,128)(2,1)S(1)}, bf16[2,40,768]{2,1,0:T(8,128)(2,1)S(1)}, u32[]{:S(2)}, u32[]{:S(2)}) %collective-permute-start.1) | collective-permute-done | bytes 122912 | tf_op jit(solution)/shard_map/ppermute | solution.py:81
  20.6 18.7 %all_gather.3 = bf16[320,768]{1,0:T(8,128)(2,1)S(1)} all-gather(bf16[80,768]{1,0:T(8,128)(2,1)S(1)} %bitcast.117), channel_id=1, replica_groups=mesh['y'=4,'g'=2,'q'=4,'zh'=2,'x'=4,'k'=2] {'q'}, dimensions={0}, use_global_device_ids=true | all-gather | bytes 614400 | tf_op jit(solution)/shard_map/all_gather | solution.py:83
  39.2 7.2 %collective-permute-start.4 = (bf16[320,768]{1,0:T(8,128)(2,1)S(1)}, bf16[320,768]{1,0:T(8,128)(2,1)S(1)}, u32[]{:S(2)}, u32[]{:S(2)}) collective-permute-start(bf16[320,768]{1,0:T(8,128)(2,1)S(1)} %all_gather.3), channel_id=1, source_target_pairs={{0,384},{128,0},{256,128},{384,256},{1,385},{129,1},{257,129},{385... | collective-permute-start | bytes 1474568 | tf_op jit(solution)/shard_map/ppermute | solution.py:55
  46.5 1.9 %collective-permute-start.2 = (bf16[320,768]{1,0:T(8,128)(2,1)S(1)}, bf16[320,768]{1,0:T(8,128)(2,1)S(1)}, u32[]{:S(2)}, u32[]{:S(2)}) collective-permute-start(bf16[320,768]{1,0:T(8,128)(2,1)S(1)} %all_gather.3), channel_id=1, source_target_pairs={{0,128},{128,256},{256,384},{384,0},{1,129},{129,257},{257,385},{3... | collective-permute-start | bytes 1474568 | tf_op jit(solution)/shard_map/ppermute | solution.py:55
  48.4 19.1 %collective-permute-start.7 = (bf16[2,40,384]{2,1,0:T(8,128)(2,1)S(1)}, bf16[2,40,384]{2,1,0:T(8,128)(2,1)S(1)}, u32[]{:S(2)}, u32[]{:S(2)}) collective-permute-start(bf16[2,40,384]{2,1,0:T(8,128)(2,1)S(1)} %slice_select_fusion), channel_id=1, source_target_pairs={{0,8},{8,0},{1,9},{9,1},{2,10},{10,2},{3,11},{11,3},{4,12},{12,4},... | collective-permute-start | bytes 184328 | tf_op jit(solution)/shard_map/ppermute | solution.py:14
  67.6 3.1 %collective-permute-start.5 = (bf16[160,768]{1,0:T(8,128)(2,1)S(1)}, bf16[160,768]{1,0:T(8,128)(2,1)S(1)}, u32[]{:S(2)}, u32[]{:S(2)}) collective-permute-start(bf16[160,768]{1,0:T(8,128)(2,1)S(1)} %slice.55), channel_id=1, source_target_pairs={{0,384},{128,0},{256,128},{384,256},{1,385},{129,1},{257,129},{385... | collective-permute-start | bytes 737288 | tf_op jit(solution)/shard_map/ppermute | solution.py:55
  70.8 2.2 %collective-permute-start.3 = (bf16[160,768]{1,0:T(8,128)(2,1)S(1)}, bf16[160,768]{1,0:T(8,128)(2,1)S(1)}, u32[]{:S(2)}, u32[]{:S(2)}) collective-permute-start(bf16[160,768]{1,0:T(8,128)(2,1)S(1)} %slice.54), channel_id=1, source_target_pairs={{0,128},{128,256},{256,384},{384,0},{1,129},{129,257},{257,385},{3... | collective-permute-start | bytes 737288 | tf_op jit(solution)/shard_map/ppermute | solution.py:55
  73.0 2.5 %collective-permute-start.10 = (bf16[2,2,40,384]{3,2,1,0:T(8,128)(2,1)S(1)}, bf16[2,2,40,384]{3,2,1,0:T(8,128)(2,1)S(1)}, u32[]{:S(2)}, u32[]{:S(2)}) collective-permute-start(bf16[2,2,40,384]{3,2,1,0:T(8,128)(2,1)S(1)} %get-tuple-element.43), channel_id=1, source_target_pairs={{0,6},{2,0},{4,2},{6,4},{1,7},{3,1},{5,3},{7,5},{8,14},{10,8},{12,... | collective-permute-start | bytes 368648 | tf_op jit(solution)/shard_map/ppermute | solution.py:55
  75.5 3.2 %collective-permute-start.9 = (bf16[2,2,40,384]{3,2,1,0:T(8,128)(2,1)S(1)}, bf16[2,2,40,384]{3,2,1,0:T(8,128)(2,1)}, u32[]{:S(2)}, u32[]{:S(2)}) collective-permute-start(bf16[2,2,40,384]{3,2,1,0:T(8,128)(2,1)S(1)} %get-tuple-element.43), channel_id=1, source_target_pairs={{0,4},{2,6},{4,0},{6,2},{1,5},{3,7},{5,1},{7,3},{8,12},{10,14},{12... | collective-permute-start | bytes 368648 | tf_op jit(solution)/shard_map/ppermute | solution.py:55
  78.8 1.9 %collective-permute-start.8 = (bf16[2,2,40,384]{3,2,1,0:T(8,128)(2,1)S(1)}, bf16[2,2,40,384]{3,2,1,0:T(8,128)(2,1)}, u32[]{:S(2)}, u32[]{:S(2)}) collective-permute-start(bf16[2,2,40,384]{3,2,1,0:T(8,128)(2,1)S(1)} %get-tuple-element.43), channel_id=1, source_target_pairs={{0,2},{2,4},{4,6},{6,0},{1,3},{3,5},{5,7},{7,1},{8,10},{10,12},{12... | collective-permute-start | bytes 368648 | tf_op jit(solution)/shard_map/ppermute | solution.py:55
  81.3 1.0 fusion
  82.6 6.5 %collective-permute-start.6 = (bf16[640,384]{0,1:T(8,128)(2,1)S(1)}, bf16[640,384]{0,1:T(8,128)(2,1)S(1)}, u32[]{:S(2)}, u32[]{:S(2)}) collective-permute-start(bf16[640,384]{0,1:T(8,128)(2,1)S(1)} %fusion), channel_id=1, source_target_pairs={{0,1},{1,0},{2,3},{3,2},{4,5},{5,4},{6,7},{7,6},{8,9},{9,8},{10,11... | collective-permute-start | bytes 1474568 | tf_op jit(solution)/shard_map/ppermute | solution.py:14
  89.2 1.2 pad_maximum_fusion.2
  90.8 1.0 add_convert_fusion
  92.4 1.0 copy.83
  93.4 5.9 %all-to-all-start = ((bf16[16,2,12,384]{3,1,2,0:T(2,128)(2,1)}), bf16[16,2,12,384]{3,1,2,0:T(2,128)(2,1)S(1)}, u32[]{:S(2)}, u32[]{:S(2)}) async-start(bf16[16,2,12,384]{3,1,2,0:T(2,128)(2,1)} %bitcast.29), calls=%async_computation | async-start | bytes 589824 | tf_op jit(solution)/shard_map/all_to_all | solution.py:102
  99.7 2.4 %collective-permute-start.11 = (bf16[2,80,384]{2,1,0:T(8,128)(2,1)S(1)}, bf16[2,80,384]{2,1,0:T(8,128)(2,1)S(1)}, u32[]{:S(2)}, u32[]{:S(2)}) collective-permute-start(bf16[2,80,384]{2,1,0:T(8,128)(2,1)S(1)} %get-tuple-element.34), channel_id=1, source_target_pairs={{0,2},{2,4},{4,6},{6,0},{1,3},{3,5},{5,7},{7,1},{8,10},{10,12},{12... | collective-permute-start | bytes 368648 | tf_op jit(solution)/shard_map/ppermute | solution.py:55
  102.2 4.0 %collective-permute-start.12 = (bf16[2,80,384]{2,1,0:T(8,128)(2,1)S(1)}, bf16[2,80,384]{2,1,0:T(8,128)(2,1)S(1)}, u32[]{:S(2)}, u32[]{:S(2)}) collective-permute-start(bf16[2,80,384]{2,1,0:T(8,128)(2,1)S(1)} %get-tuple-element.33), channel_id=1, source_target_pairs={{0,6},{2,0},{4,2},{6,4},{1,7},{3,1},{5,3},{7,5},{8,14},{10,8},{12,... | collective-permute-start | bytes 368648 | tf_op jit(solution)/shard_map/ppermute | solution.py:55
  106.2 3.9 %collective-permute-start.13 = (bf16[2,80,384]{2,1,0:T(8,128)(2,1)S(1)}, bf16[2,80,384]{2,1,0:T(8,128)(2,1)S(1)}, u32[]{:S(2)}, u32[]{:S(2)}) collective-permute-start(bf16[2,80,384]{2,1,0:T(8,128)(2,1)S(1)} %get-tuple-element.32), channel_id=1, source_target_pairs={{0,4},{2,6},{4,0},{6,2},{1,5},{3,7},{5,1},{7,3},{8,12},{10,14},{12... | collective-permute-start | bytes 368648 | tf_op jit(solution)/shard_map/ppermute | solution.py:55
  110.4 2.9 %collective-permute-done.13 = bf16[2,80,384]{2,1,0:T(8,128)(2,1)S(1)} collective-permute-done((bf16[2,80,384]{2,1,0:T(8,128)(2,1)S(1)}, bf16[2,80,384]{2,1,0:T(8,128)(2,1)S(1)}, u32[]{:S(2)}, u32[]{:S(2)}) %collective-permute-start.13) | collective-permute-done | bytes 122912 | tf_op jit(solution)/shard_map/ppermute | solution.py:55
  113.4 4.5 %collective-permute-start.14 = (bf16[2,40,384]{2,1,0:T(8,128)(2,1)S(1)}, bf16[2,40,384]{2,1,0:T(8,128)(2,1)S(1)}, u32[]{:S(2)}, u32[]{:S(2)}) collective-permute-start(bf16[2,40,384]{2,1,0:T(8,128)(2,1)S(1)} %select_bitcast_fusion), channel_id=1, source_target_pairs={{0,1},{1,0},{2,3},{3,2},{4,5},{5,4},{6,7},{7,6},{8,9},{9,8},{10,11... | collective-permute-start | bytes 184328 | tf_op jit(solution)/shard_map/ppermute | solution.py:14
  118.6 7.7 %all-to-all-start.1 = ((bf16[4,12,384]{2,1,0:T(8,128)(2,1)}), bf16[4,12,384]{2,1,0:T(8,128)(2,1)S(1)}, u32[]{:S(2)}, u32[]{:S(2)}) async-start(bf16[4,12,384]{2,1,0:T(8,128)(2,1)} %bitcast.41), calls=%async_computation.1 | async-start | bytes 98304 | tf_op jit(solution)/shard_map/all_to_all | solution.py:115
  126.4 12.1 %collective-permute-start.15 = (bf16[2,40,384]{2,1,0:T(8,128)(2,1)S(1)}, bf16[2,40,384]{2,1,0:T(8,128)(2,1)S(1)}, u32[]{:S(2)}, u32[]{:S(2)}) collective-permute-start(bf16[2,40,384]{2,1,0:T(8,128)(2,1)S(1)} %fusion.5), channel_id=1, source_target_pairs={{0,8},{8,0},{1,9},{9,1},{2,10},{10,2},{3,11},{11,3},{4,12},{12,4},... | collective-permute-start | bytes 184328 | tf_op jit(solution)/shard_map/ppermute | solution.py:14
  138.5 0.7 broadcast_in_dim.50
  139.2 4.8 %all-to-all-start.2 = ((bf16[8,12,384]{2,1,0:T(8,128)(2,1)}), bf16[8,12,384]{2,1,0:T(8,128)(2,1)S(1)}, u32[]{:S(2)}, u32[]{:S(2)}) async-start(bf16[8,12,384]{2,1,0:T(8,128)(2,1)} %broadcast_in_dim.50), calls=%async_computation.2 | async-start | bytes 196608 | tf_op jit(solution)/shard_map/all_to_all | solution.py:27
  144.0 0.7 copy.95
  144.7 4.3 %all-to-all-done.2 = bf16[8,12,384]{2,1,0:T(8,128)(2,1)S(1)} async-done(((bf16[8,12,384]{2,1,0:T(8,128)(2,1)}), bf16[8,12,384]{2,1,0:T(8,128)(2,1)S(1)}, u32[]{:S(2)}, u32[]{:S(2)}) %all-to-all-start.2) | async-done | bytes 73760 | tf_op jit(solution)/shard_map/all_to_all | solution.py:27
  149.2 0.6 copy.96
  (61 shorter events, 4.0 us)
Async XLA Ops:
  0.6 80.7 %copy-start = (bf16[640,1280]{1,0:T(8,128)(2,1)S(1)}, bf16[640,1280]{1,0:T(8,128)(2,1)}, u32[]{:S(2)}) copy-start(bf16[640,1280]{1,0:T(8,128)(2,1)} %param.4) | copy-start | bytes 4915204
  1.6 10.2 %collective-permute-start = (bf16[40,768]{1,0:T(8,128)(2,1)S(1)}, bf16[40,768]{1,0:T(8,128)(2,1)S(1)}, u32[]{:S(2)}, u32[]{:S(2)}) collective-permute-start(bf16[40,768]{1,0:T(8,128)(2,1)S(1)} %bitcast.118), channel_id=1, source_target_pairs={{0,1},{1,0},{2,3},{3,2},{4,5},{5,4},{6,7},{7,6},{8,9},{9,8},{10,11... | collective-permute-start | bytes 184328 | tf_op jit(solution)/shard_map/ppermute | solution.py:14
  11.9 8.7 %collective-permute-start.1 = (bf16[2,40,768]{2,1,0:T(8,128)(2,1)S(1)}, bf16[2,40,768]{2,1,0:T(8,128)(2,1)S(1)}, u32[]{:S(2)}, u32[]{:S(2)}) collective-permute-start(bf16[2,40,768]{2,1,0:T(8,128)(2,1)S(1)} %maximum_multiply_fusion), channel_id=1, source_target_pairs={{0,0},{1,64},{2,16},{3,80},{4,32},{5,96},{6,48},{7,112},{8,128},{9... | collective-permute-start | bytes 368648 | tf_op jit(solution)/shard_map/ppermute | solution.py:81
  39.2 28.3 %collective-permute-start.4 = (bf16[320,768]{1,0:T(8,128)(2,1)S(1)}, bf16[320,768]{1,0:T(8,128)(2,1)S(1)}, u32[]{:S(2)}, u32[]{:S(2)}) collective-permute-start(bf16[320,768]{1,0:T(8,128)(2,1)S(1)} %all_gather.3), channel_id=1, source_target_pairs={{0,384},{128,0},{256,128},{384,256},{1,385},{129,1},{257,129},{385... | collective-permute-start | bytes 1474568 | tf_op jit(solution)/shard_map/ppermute | solution.py:55
  46.5 24.3 %collective-permute-start.2 = (bf16[320,768]{1,0:T(8,128)(2,1)S(1)}, bf16[320,768]{1,0:T(8,128)(2,1)S(1)}, u32[]{:S(2)}, u32[]{:S(2)}) collective-permute-start(bf16[320,768]{1,0:T(8,128)(2,1)S(1)} %all_gather.3), channel_id=1, source_target_pairs={{0,128},{128,256},{256,384},{384,0},{1,129},{129,257},{257,385},{3... | collective-permute-start | bytes 1474568 | tf_op jit(solution)/shard_map/ppermute | solution.py:55
  48.4 24.5 %collective-permute-start.7 = (bf16[2,40,384]{2,1,0:T(8,128)(2,1)S(1)}, bf16[2,40,384]{2,1,0:T(8,128)(2,1)S(1)}, u32[]{:S(2)}, u32[]{:S(2)}) collective-permute-start(bf16[2,40,384]{2,1,0:T(8,128)(2,1)S(1)} %slice_select_fusion), channel_id=1, source_target_pairs={{0,8},{8,0},{1,9},{9,1},{2,10},{10,2},{3,11},{11,3},{4,12},{12,4},... | collective-permute-start | bytes 184328 | tf_op jit(solution)/shard_map/ppermute | solution.py:14
  67.6 13.1 %collective-permute-start.5 = (bf16[160,768]{1,0:T(8,128)(2,1)S(1)}, bf16[160,768]{1,0:T(8,128)(2,1)S(1)}, u32[]{:S(2)}, u32[]{:S(2)}) collective-permute-start(bf16[160,768]{1,0:T(8,128)(2,1)S(1)} %slice.55), channel_id=1, source_target_pairs={{0,384},{128,0},{256,128},{384,256},{1,385},{129,1},{257,129},{385... | collective-permute-start | bytes 737288 | tf_op jit(solution)/shard_map/ppermute | solution.py:55
  70.8 9.9 %collective-permute-start.3 = (bf16[160,768]{1,0:T(8,128)(2,1)S(1)}, bf16[160,768]{1,0:T(8,128)(2,1)S(1)}, u32[]{:S(2)}, u32[]{:S(2)}) collective-permute-start(bf16[160,768]{1,0:T(8,128)(2,1)S(1)} %slice.54), channel_id=1, source_target_pairs={{0,128},{128,256},{256,384},{384,0},{1,129},{129,257},{257,385},{3... | collective-permute-start | bytes 737288 | tf_op jit(solution)/shard_map/ppermute | solution.py:55
  73.0 16.2 %collective-permute-start.10 = (bf16[2,2,40,384]{3,2,1,0:T(8,128)(2,1)S(1)}, bf16[2,2,40,384]{3,2,1,0:T(8,128)(2,1)S(1)}, u32[]{:S(2)}, u32[]{:S(2)}) collective-permute-start(bf16[2,2,40,384]{3,2,1,0:T(8,128)(2,1)S(1)} %get-tuple-element.43), channel_id=1, source_target_pairs={{0,6},{2,0},{4,2},{6,4},{1,7},{3,1},{5,3},{7,5},{8,14},{10,8},{12,... | collective-permute-start | bytes 368648 | tf_op jit(solution)/shard_map/ppermute | solution.py:55
  75.5 13.7 %collective-permute-start.9 = (bf16[2,2,40,384]{3,2,1,0:T(8,128)(2,1)S(1)}, bf16[2,2,40,384]{3,2,1,0:T(8,128)(2,1)}, u32[]{:S(2)}, u32[]{:S(2)}) collective-permute-start(bf16[2,2,40,384]{3,2,1,0:T(8,128)(2,1)S(1)} %get-tuple-element.43), channel_id=1, source_target_pairs={{0,4},{2,6},{4,0},{6,2},{1,5},{3,7},{5,1},{7,3},{8,12},{10,14},{12... | collective-permute-start | bytes 368648 | tf_op jit(solution)/shard_map/ppermute | solution.py:55
  78.8 10.5 %collective-permute-start.8 = (bf16[2,2,40,384]{3,2,1,0:T(8,128)(2,1)S(1)}, bf16[2,2,40,384]{3,2,1,0:T(8,128)(2,1)}, u32[]{:S(2)}, u32[]{:S(2)}) collective-permute-start(bf16[2,2,40,384]{3,2,1,0:T(8,128)(2,1)S(1)} %get-tuple-element.43), channel_id=1, source_target_pairs={{0,2},{2,4},{4,6},{6,0},{1,3},{3,5},{5,7},{7,1},{8,10},{10,12},{12... | collective-permute-start | bytes 368648 | tf_op jit(solution)/shard_map/ppermute | solution.py:55
  81.3 1.3 copy-start.1
  82.6 8.0 %collective-permute-start.6 = (bf16[640,384]{0,1:T(8,128)(2,1)S(1)}, bf16[640,384]{0,1:T(8,128)(2,1)S(1)}, u32[]{:S(2)}, u32[]{:S(2)}) collective-permute-start(bf16[640,384]{0,1:T(8,128)(2,1)S(1)} %fusion), channel_id=1, source_target_pairs={{0,1},{1,0},{2,3},{3,2},{4,5},{5,4},{6,7},{7,6},{8,9},{9,8},{10,11... | collective-permute-start | bytes 1474568 | tf_op jit(solution)/shard_map/ppermute | solution.py:14
  89.2 1.7 %copy-start.2 = (bf16[1280,768]{1,0:T(8,128)(2,1)S(1)}, bf16[1280,768]{1,0:T(8,128)(2,1)}, u32[]{:S(2)}) copy-start(bf16[1280,768]{1,0:T(8,128)(2,1)} %copy-done.1) | copy-start | bytes 5898244
  93.4 16.7 %all-to-all-start = ((bf16[16,2,12,384]{3,1,2,0:T(2,128)(2,1)}), bf16[16,2,12,384]{3,1,2,0:T(2,128)(2,1)S(1)}, u32[]{:S(2)}, u32[]{:S(2)}) async-start(bf16[16,2,12,384]{3,1,2,0:T(2,128)(2,1)} %bitcast.29), calls=%async_computation | async-start | bytes 589824 | tf_op jit(solution)/shard_map/all_to_all | solution.py:102
  99.7 49.4 %copy-start.3 = (f32[2,12,384]{2,0,1:T(2,128)S(1)}, f32[2,12,384]{2,0,1:T(2,128)}, u32[]{:S(2)}) copy-start(f32[2,12,384]{2,0,1:T(2,128)} %param.7) | copy-start | bytes 110596
  99.7 10.7 %collective-permute-start.11 = (bf16[2,80,384]{2,1,0:T(8,128)(2,1)S(1)}, bf16[2,80,384]{2,1,0:T(8,128)(2,1)S(1)}, u32[]{:S(2)}, u32[]{:S(2)}) collective-permute-start(bf16[2,80,384]{2,1,0:T(8,128)(2,1)S(1)} %get-tuple-element.34), channel_id=1, source_target_pairs={{0,2},{2,4},{4,6},{6,0},{1,3},{3,5},{5,7},{7,1},{8,10},{10,12},{12... | collective-permute-start | bytes 368648 | tf_op jit(solution)/shard_map/ppermute | solution.py:55
  102.2 8.2 %collective-permute-start.12 = (bf16[2,80,384]{2,1,0:T(8,128)(2,1)S(1)}, bf16[2,80,384]{2,1,0:T(8,128)(2,1)S(1)}, u32[]{:S(2)}, u32[]{:S(2)}) collective-permute-start(bf16[2,80,384]{2,1,0:T(8,128)(2,1)S(1)} %get-tuple-element.33), channel_id=1, source_target_pairs={{0,6},{2,0},{4,2},{6,4},{1,7},{3,1},{5,3},{7,5},{8,14},{10,8},{12,... | collective-permute-start | bytes 368648 | tf_op jit(solution)/shard_map/ppermute | solution.py:55
  106.2 7.1 %collective-permute-start.13 = (bf16[2,80,384]{2,1,0:T(8,128)(2,1)S(1)}, bf16[2,80,384]{2,1,0:T(8,128)(2,1)S(1)}, u32[]{:S(2)}, u32[]{:S(2)}) collective-permute-start(bf16[2,80,384]{2,1,0:T(8,128)(2,1)S(1)} %get-tuple-element.32), channel_id=1, source_target_pairs={{0,4},{2,6},{4,0},{6,2},{1,5},{3,7},{5,1},{7,3},{8,12},{10,14},{12... | collective-permute-start | bytes 368648 | tf_op jit(solution)/shard_map/ppermute | solution.py:55
  113.4 12.9 %collective-permute-start.14 = (bf16[2,40,384]{2,1,0:T(8,128)(2,1)S(1)}, bf16[2,40,384]{2,1,0:T(8,128)(2,1)S(1)}, u32[]{:S(2)}, u32[]{:S(2)}) collective-permute-start(bf16[2,40,384]{2,1,0:T(8,128)(2,1)S(1)} %select_bitcast_fusion), channel_id=1, source_target_pairs={{0,1},{1,0},{2,3},{3,2},{4,5},{5,4},{6,7},{7,6},{8,9},{9,8},{10,11... | collective-permute-start | bytes 184328 | tf_op jit(solution)/shard_map/ppermute | solution.py:14
  118.6 19.9 %all-to-all-start.1 = ((bf16[4,12,384]{2,1,0:T(8,128)(2,1)}), bf16[4,12,384]{2,1,0:T(8,128)(2,1)S(1)}, u32[]{:S(2)}, u32[]{:S(2)}) async-start(bf16[4,12,384]{2,1,0:T(8,128)(2,1)} %bitcast.41), calls=%async_computation.1 | async-start | bytes 98304 | tf_op jit(solution)/shard_map/all_to_all | solution.py:115
  126.4 17.6 %collective-permute-start.15 = (bf16[2,40,384]{2,1,0:T(8,128)(2,1)S(1)}, bf16[2,40,384]{2,1,0:T(8,128)(2,1)S(1)}, u32[]{:S(2)}, u32[]{:S(2)}) collective-permute-start(bf16[2,40,384]{2,1,0:T(8,128)(2,1)S(1)} %fusion.5), channel_id=1, source_target_pairs={{0,8},{8,0},{1,9},{9,1},{2,10},{10,2},{3,11},{11,3},{4,12},{12,4},... | collective-permute-start | bytes 184328 | tf_op jit(solution)/shard_map/ppermute | solution.py:14
  139.2 9.8 %all-to-all-start.2 = ((bf16[8,12,384]{2,1,0:T(8,128)(2,1)}), bf16[8,12,384]{2,1,0:T(8,128)(2,1)S(1)}, u32[]{:S(2)}, u32[]{:S(2)}) async-start(bf16[8,12,384]{2,1,0:T(8,128)(2,1)} %broadcast_in_dim.50), calls=%async_computation.2 | async-start | bytes 196608 | tf_op jit(solution)/shard_map/all_to_all | solution.py:27

commit v4 on v3

--- a/solution.py
+++ b/solution.py
@@ -33,16 +33,14 @@
 
 def masked_pair(lower_panel, structure, k):
     rows = lower_panel.shape[0]
-    flat = lower_panel.reshape(rows, 768)
-    pair = ordered(flat, swapped(flat, "k"), k)
+    pair = ordered(lower_panel, swapped(lower_panel, "k"), k)
     start = (lax.axis_index(ROW) * 16 + lax.axis_index(COL) - k) * rows
     block = start // BS
     here = lax.dynamic_slice_in_dim(structure, block, 1, 0)
     after_it = lax.dynamic_slice_in_dim(structure, jnp.minimum(block + 1, structure.shape[0] - 1), 1, 0)
     row = start + lax.broadcasted_iota(jnp.int32, (2 * rows, 1), 0)
     keep = jnp.where(row < (block + 1) * BS, here, after_it).astype(jnp.bfloat16)
-    keep = jnp.repeat(keep, 384, axis=1).reshape(2, rows, 768)
-    return pair * keep
+    return (pair * keep.reshape(2, rows, 2, 1)).reshape(2, rows, 768)
 
 def added(parts):
     return jnp.sum(parts.astype(jnp.float32), axis=0)

time: 151 us -> 151 us (level)
  no operation moved by 1% of the time
where the time goes in v4:
time: 151 us; the launch traced here: 150 us
  starting transfers between devices  105 us (70%)
  blocking collectives  18.6 us (12%)
  waiting for transfers between devices  12.5 us (8%)
  local copies, waits for them, and re-layouts  6.24 us (4%)
  other arithmetic  3.23 us (2%)
  matrix products  2.47 us (2%)
    ppermute x5, starting transfers between devices, swapped(): return lax.ppermute(x, axis, [(0, 1), (1, 0)])  50.9 us
    ppermute x10, starting transfers between devices, turned(): return lax.ppermute(x, axis, [(i, (i + d) % n) for i in range(n)])  32.7 us
    all_gather x1, blocking collectives, shards(): quarter = lax.all_gather(moved.reshape(80, 768), 'q', tiled=True)  18.6 us
    all_to_all x1, starting transfers between devices, shards(): by_z = added(lax.all_to_all(by_z, ('g', 'zh'), 0, 0)).astype(bf16)  7.75 us
    all_to_all x1, starting transfers between devices, shards(): lax.all_to_all(by_yq.reshape(16, 2, 12, 384), ('y', 'q'), 0, 0)  5.89 us
    ppermute x1, waiting for transfers between devices, shards(): moved = lax.ppermute(pair, AXES, to_columns())  5.26 us
    all_to_all x1, starting transfers between devices, gathered(): return lax.all_to_all(jnp.broadcast_to(x[None], (n,) + x.shape), axis, 0, 0)  4.85 us
    all_to_all x1, waiting for transfers between devices, gathered(): return lax.all_to_all(jnp.broadcast_to(x[None], (n,) + x.shape), axis, 0, 0)  4.29 us
  transfers between devices with their start and end apart: 19, of which 3 were waited for; matrix products, arithmetic and copies ran while one was open for 5% of the time, Pallas kernels for 0%

profile of v4, /device:TPU:1, one launch (start us, length us, event | category | flops | bytes accessed | tf_op | source)
XLA Modules:
  0.0 150.0 jit_solution(8879503128483235014)
XLA Ops:
  0.6 8.9 %collective-permute-start = (bf16[40,2,384]{2,1,0:T(2,128)(2,1)}, bf16[40,2,384]{2,1,0:T(2,128)(2,1)S(1)}, u32[]{:S(2)}, u32[]{:S(2)}) collective-permute-start(bf16[40,2,384]{2,1,0:T(2,128)(2,1)} %param.5), channel_id=1, source_target_pairs={{0,1},{1,0},{2,3},{3,2},{4,5},{5,4},{6,7},{7,6},{8,9},{9,8},{10,11... | collective-permute-start | bytes 184328 | tf_op jit(solution)/shard_map/ppermute | solution.py:14
  9.7 1.0 fusion.9
  11.0 0.8 broadcast_select_fusion.1
  12.0 3.4 %collective-permute-start.1 = (bf16[2,40,768]{2,1,0:T(8,128)(2,1)S(1)}, bf16[2,40,768]{2,1,0:T(8,128)(2,1)S(1)}, u32[]{:S(2)}, u32[]{:S(2)}) collective-permute-start(bf16[2,40,768]{2,1,0:T(8,128)(2,1)S(1)} %maximum_multiply_fusion), channel_id=1, source_target_pairs={{0,0},{1,64},{2,16},{3,80},{4,32},{5,96},{6,48},{7,112},{8,128},{9... | collective-permute-start | bytes 368648 | tf_op jit(solution)/shard_map/ppermute | solution.py:79
  15.3 5.3 %collective-permute-done.1 = bf16[2,40,768]{2,1,0:T(8,128)(2,1)S(1)} collective-permute-done((bf16[2,40,768]{2,1,0:T(8,128)(2,1)S(1)}, bf16[2,40,768]{2,1,0:T(8,128)(2,1)S(1)}, u32[]{:S(2)}, u32[]{:S(2)}) %collective-permute-start.1) | collective-permute-done | bytes 122912 | tf_op jit(solution)/shard_map/ppermute | solution.py:79
  20.6 18.6 %all_gather.3 = bf16[320,768]{1,0:T(8,128)(2,1)S(1)} all-gather(bf16[80,768]{1,0:T(8,128)(2,1)S(1)} %bitcast.115), channel_id=1, replica_groups=mesh['y'=4,'g'=2,'q'=4,'zh'=2,'x'=4,'k'=2] {'q'}, dimensions={0}, use_global_device_ids=true | all-gather | bytes 614400 | tf_op jit(solution)/shard_map/all_gather | solution.py:81
  39.3 7.3 %collective-permute-start.4 = (bf16[320,768]{1,0:T(8,128)(2,1)S(1)}, bf16[320,768]{1,0:T(8,128)(2,1)S(1)}, u32[]{:S(2)}, u32[]{:S(2)}) collective-permute-start(bf16[320,768]{1,0:T(8,128)(2,1)S(1)} %all_gather.3), channel_id=1, source_target_pairs={{0,384},{128,0},{256,128},{384,256},{1,385},{129,1},{257,129},{385... | collective-permute-start | bytes 1474568 | tf_op jit(solution)/shard_map/ppermute | solution.py:53
  46.6 1.9 %collective-permute-start.2 = (bf16[320,768]{1,0:T(8,128)(2,1)S(1)}, bf16[320,768]{1,0:T(8,128)(2,1)S(1)}, u32[]{:S(2)}, u32[]{:S(2)}) collective-permute-start(bf16[320,768]{1,0:T(8,128)(2,1)S(1)} %all_gather.3), channel_id=1, source_target_pairs={{0,128},{128,256},{256,384},{384,0},{1,129},{129,257},{257,385},{3... | collective-permute-start | bytes 1474568 | tf_op jit(solution)/shard_map/ppermute | solution.py:53
  48.6 19.0 %collective-permute-start.7 = (bf16[2,40,384]{2,1,0:T(8,128)(2,1)S(1)}, bf16[2,40,384]{2,1,0:T(8,128)(2,1)S(1)}, u32[]{:S(2)}, u32[]{:S(2)}) collective-permute-start(bf16[2,40,384]{2,1,0:T(8,128)(2,1)S(1)} %slice_select_fusion), channel_id=1, source_target_pairs={{0,8},{8,0},{1,9},{9,1},{2,10},{10,2},{3,11},{11,3},{4,12},{12,4},... | collective-permute-start | bytes 184328 | tf_op jit(solution)/shard_map/ppermute | solution.py:14
  67.7 3.1 %collective-permute-start.5 = (bf16[160,768]{1,0:T(8,128)(2,1)S(1)}, bf16[160,768]{1,0:T(8,128)(2,1)S(1)}, u32[]{:S(2)}, u32[]{:S(2)}) collective-permute-start(bf16[160,768]{1,0:T(8,128)(2,1)S(1)} %slice.55), channel_id=1, source_target_pairs={{0,384},{128,0},{256,128},{384,256},{1,385},{129,1},{257,129},{385... | collective-permute-start | bytes 737288 | tf_op jit(solution)/shard_map/ppermute | solution.py:53
  70.9 2.2 %collective-permute-start.3 = (bf16[160,768]{1,0:T(8,128)(2,1)S(1)}, bf16[160,768]{1,0:T(8,128)(2,1)S(1)}, u32[]{:S(2)}, u32[]{:S(2)}) collective-permute-start(bf16[160,768]{1,0:T(8,128)(2,1)S(1)} %slice.54), channel_id=1, source_target_pairs={{0,128},{128,256},{256,384},{384,0},{1,129},{129,257},{257,385},{3... | collective-permute-start | bytes 737288 | tf_op jit(solution)/shard_map/ppermute | solution.py:53
  73.1 2.4 %collective-permute-start.10 = (bf16[2,2,40,384]{3,2,1,0:T(8,128)(2,1)S(1)}, bf16[2,2,40,384]{3,2,1,0:T(8,128)(2,1)S(1)}, u32[]{:S(2)}, u32[]{:S(2)}) collective-permute-start(bf16[2,2,40,384]{3,2,1,0:T(8,128)(2,1)S(1)} %get-tuple-element.43), channel_id=1, source_target_pairs={{0,6},{2,0},{4,2},{6,4},{1,7},{3,1},{5,3},{7,5},{8,14},{10,8},{12,... | collective-permute-start | bytes 368648 | tf_op jit(solution)/shard_map/ppermute | solution.py:53
  75.6 3.4 %collective-permute-start.9 = (bf16[2,2,40,384]{3,2,1,0:T(8,128)(2,1)S(1)}, bf16[2,2,40,384]{3,2,1,0:T(8,128)(2,1)}, u32[]{:S(2)}, u32[]{:S(2)}) collective-permute-start(bf16[2,2,40,384]{3,2,1,0:T(8,128)(2,1)S(1)} %get-tuple-element.43), channel_id=1, source_target_pairs={{0,4},{2,6},{4,0},{6,2},{1,5},{3,7},{5,1},{7,3},{8,12},{10,14},{12... | collective-permute-start | bytes 368648 | tf_op jit(solution)/shard_map/ppermute | solution.py:53
  79.0 1.9 %collective-permute-start.8 = (bf16[2,2,40,384]{3,2,1,0:T(8,128)(2,1)S(1)}, bf16[2,2,40,384]{3,2,1,0:T(8,128)(2,1)}, u32[]{:S(2)}, u32[]{:S(2)}) collective-permute-start(bf16[2,2,40,384]{3,2,1,0:T(8,128)(2,1)S(1)} %get-tuple-element.43), channel_id=1, source_target_pairs={{0,2},{2,4},{4,6},{6,0},{1,3},{3,5},{5,7},{7,1},{8,10},{10,12},{12... | collective-permute-start | bytes 368648 | tf_op jit(solution)/shard_map/ppermute | solution.py:53
  81.5 1.0 fusion
  82.8 6.4 %collective-permute-start.6 = (bf16[640,384]{0,1:T(8,128)(2,1)S(1)}, bf16[640,384]{0,1:T(8,128)(2,1)S(1)}, u32[]{:S(2)}, u32[]{:S(2)}) collective-permute-start(bf16[640,384]{0,1:T(8,128)(2,1)S(1)} %fusion), channel_id=1, source_target_pairs={{0,1},{1,0},{2,3},{3,2},{4,5},{5,4},{6,7},{7,6},{8,9},{9,8},{10,11... | collective-permute-start | bytes 1474568 | tf_op jit(solution)/shard_map/ppermute | solution.py:14
  89.3 1.2 pad_maximum_fusion.2
  90.9 1.0 add_convert_fusion
  92.5 1.0 copy.83
  93.5 5.9 %all-to-all-start = ((bf16[16,2,12,384]{3,1,2,0:T(2,128)(2,1)}), bf16[16,2,12,384]{3,1,2,0:T(2,128)(2,1)S(1)}, u32[]{:S(2)}, u32[]{:S(2)}) async-start(bf16[16,2,12,384]{3,1,2,0:T(2,128)(2,1)} %bitcast.27), calls=%async_computation | async-start | bytes 589824 | tf_op jit(solution)/shard_map/all_to_all | solution.py:100
  99.8 2.4 %collective-permute-start.11 = (bf16[2,80,384]{2,1,0:T(8,128)(2,1)S(1)}, bf16[2,80,384]{2,1,0:T(8,128)(2,1)S(1)}, u32[]{:S(2)}, u32[]{:S(2)}) collective-permute-start(bf16[2,80,384]{2,1,0:T(8,128)(2,1)S(1)} %get-tuple-element.34), channel_id=1, source_target_pairs={{0,2},{2,4},{4,6},{6,0},{1,3},{3,5},{5,7},{7,1},{8,10},{10,12},{12... | collective-permute-start | bytes 368648 | tf_op jit(solution)/shard_map/ppermute | solution.py:53
  102.3 4.1 %collective-permute-start.12 = (bf16[2,80,384]{2,1,0:T(8,128)(2,1)S(1)}, bf16[2,80,384]{2,1,0:T(8,128)(2,1)S(1)}, u32[]{:S(2)}, u32[]{:S(2)}) collective-permute-start(bf16[2,80,384]{2,1,0:T(8,128)(2,1)S(1)} %get-tuple-element.33), channel_id=1, source_target_pairs={{0,6},{2,0},{4,2},{6,4},{1,7},{3,1},{5,3},{7,5},{8,14},{10,8},{12,... | collective-permute-start | bytes 368648 | tf_op jit(solution)/shard_map/ppermute | solution.py:53
  106.3 3.9 %collective-permute-start.13 = (bf16[2,80,384]{2,1,0:T(8,128)(2,1)S(1)}, bf16[2,80,384]{2,1,0:T(8,128)(2,1)S(1)}, u32[]{:S(2)}, u32[]{:S(2)}) collective-permute-start(bf16[2,80,384]{2,1,0:T(8,128)(2,1)S(1)} %get-tuple-element.32), channel_id=1, source_target_pairs={{0,4},{2,6},{4,0},{6,2},{1,5},{3,7},{5,1},{7,3},{8,12},{10,14},{12... | collective-permute-start | bytes 368648 | tf_op jit(solution)/shard_map/ppermute | solution.py:53
  110.5 2.9 %collective-permute-done.13 = bf16[2,80,384]{2,1,0:T(8,128)(2,1)S(1)} collective-permute-done((bf16[2,80,384]{2,1,0:T(8,128)(2,1)S(1)}, bf16[2,80,384]{2,1,0:T(8,128)(2,1)S(1)}, u32[]{:S(2)}, u32[]{:S(2)}) %collective-permute-start.13) | collective-permute-done | bytes 122912 | tf_op jit(solution)/shard_map/ppermute | solution.py:53
  113.5 4.5 %collective-permute-start.14 = (bf16[2,40,384]{2,1,0:T(8,128)(2,1)S(1)}, bf16[2,40,384]{2,1,0:T(8,128)(2,1)S(1)}, u32[]{:S(2)}, u32[]{:S(2)}) collective-permute-start(bf16[2,40,384]{2,1,0:T(8,128)(2,1)S(1)} %select_bitcast_fusion), channel_id=1, source_target_pairs={{0,1},{1,0},{2,3},{3,2},{4,5},{5,4},{6,7},{7,6},{8,9},{9,8},{10,11... | collective-permute-start | bytes 184328 | tf_op jit(solution)/shard_map/ppermute | solution.py:14
  118.7 7.7 %all-to-all-start.1 = ((bf16[4,12,384]{2,1,0:T(8,128)(2,1)}), bf16[4,12,384]{2,1,0:T(8,128)(2,1)S(1)}, u32[]{:S(2)}, u32[]{:S(2)}) async-start(bf16[4,12,384]{2,1,0:T(8,128)(2,1)} %bitcast.39), calls=%async_computation.1 | async-start | bytes 98304 | tf_op jit(solution)/shard_map/all_to_all | solution.py:113
  126.5 12.1 %collective-permute-start.15 = (bf16[2,40,384]{2,1,0:T(8,128)(2,1)S(1)}, bf16[2,40,384]{2,1,0:T(8,128)(2,1)S(1)}, u32[]{:S(2)}, u32[]{:S(2)}) collective-permute-start(bf16[2,40,384]{2,1,0:T(8,128)(2,1)S(1)} %fusion.5), channel_id=1, source_target_pairs={{0,8},{8,0},{1,9},{9,1},{2,10},{10,2},{3,11},{11,3},{4,12},{12,4},... | collective-permute-start | bytes 184328 | tf_op jit(solution)/shard_map/ppermute | solution.py:14
  138.6 0.7 broadcast_in_dim.46
  139.3 4.9 %all-to-all-start.2 = ((bf16[8,12,384]{2,1,0:T(8,128)(2,1)}), bf16[8,12,384]{2,1,0:T(8,128)(2,1)S(1)}, u32[]{:S(2)}, u32[]{:S(2)}) async-start(bf16[8,12,384]{2,1,0:T(8,128)(2,1)} %broadcast_in_dim.46), calls=%async_computation.2 | async-start | bytes 196608 | tf_op jit(solution)/shard_map/all_to_all | solution.py:27
  144.2 0.7 copy.95
  144.8 4.3 %all-to-all-done.2 = bf16[8,12,384]{2,1,0:T(8,128)(2,1)S(1)} async-done(((bf16[8,12,384]{2,1,0:T(8,128)(2,1)}), bf16[8,12,384]{2,1,0:T(8,128)(2,1)S(1)}, u32[]{:S(2)}, u32[]{:S(2)}) %all-to-all-start.2) | async-done | bytes 73760 | tf_op jit(solution)/shard_map/all_to_all | solution.py:27
  149.3 0.6 copy.96
  (62 shorter events, 4.1 us)
Async XLA Ops:
  0.6 80.9 %copy-start = (bf16[640,1280]{1,0:T(8,128)(2,1)S(1)}, bf16[640,1280]{1,0:T(8,128)(2,1)}, u32[]{:S(2)}) copy-start(bf16[640,1280]{1,0:T(8,128)(2,1)} %param.4) | copy-start | bytes 4915204
  0.6 10.3 %collective-permute-start = (bf16[40,2,384]{2,1,0:T(2,128)(2,1)}, bf16[40,2,384]{2,1,0:T(2,128)(2,1)S(1)}, u32[]{:S(2)}, u32[]{:S(2)}) collective-permute-start(bf16[40,2,384]{2,1,0:T(2,128)(2,1)} %param.5), channel_id=1, source_target_pairs={{0,1},{1,0},{2,3},{3,2},{4,5},{5,4},{6,7},{7,6},{8,9},{9,8},{10,11... | collective-permute-start | bytes 184328 | tf_op jit(solution)/shard_map/ppermute | solution.py:14
  12.0 8.6 %collective-permute-start.1 = (bf16[2,40,768]{2,1,0:T(8,128)(2,1)S(1)}, bf16[2,40,768]{2,1,0:T(8,128)(2,1)S(1)}, u32[]{:S(2)}, u32[]{:S(2)}) collective-permute-start(bf16[2,40,768]{2,1,0:T(8,128)(2,1)S(1)} %maximum_multiply_fusion), channel_id=1, source_target_pairs={{0,0},{1,64},{2,16},{3,80},{4,32},{5,96},{6,48},{7,112},{8,128},{9... | collective-permute-start | bytes 368648 | tf_op jit(solution)/shard_map/ppermute | solution.py:79
  39.3 28.4 %collective-permute-start.4 = (bf16[320,768]{1,0:T(8,128)(2,1)S(1)}, bf16[320,768]{1,0:T(8,128)(2,1)S(1)}, u32[]{:S(2)}, u32[]{:S(2)}) collective-permute-start(bf16[320,768]{1,0:T(8,128)(2,1)S(1)} %all_gather.3), channel_id=1, source_target_pairs={{0,384},{128,0},{256,128},{384,256},{1,385},{129,1},{257,129},{385... | collective-permute-start | bytes 1474568 | tf_op jit(solution)/shard_map/ppermute | solution.py:53
  46.6 24.2 %collective-permute-start.2 = (bf16[320,768]{1,0:T(8,128)(2,1)S(1)}, bf16[320,768]{1,0:T(8,128)(2,1)S(1)}, u32[]{:S(2)}, u32[]{:S(2)}) collective-permute-start(bf16[320,768]{1,0:T(8,128)(2,1)S(1)} %all_gather.3), channel_id=1, source_target_pairs={{0,128},{128,256},{256,384},{384,0},{1,129},{129,257},{257,385},{3... | collective-permute-start | bytes 1474568 | tf_op jit(solution)/shard_map/ppermute | solution.py:53
  48.6 24.5 %collective-permute-start.7 = (bf16[2,40,384]{2,1,0:T(8,128)(2,1)S(1)}, bf16[2,40,384]{2,1,0:T(8,128)(2,1)S(1)}, u32[]{:S(2)}, u32[]{:S(2)}) collective-permute-start(bf16[2,40,384]{2,1,0:T(8,128)(2,1)S(1)} %slice_select_fusion), channel_id=1, source_target_pairs={{0,8},{8,0},{1,9},{9,1},{2,10},{10,2},{3,11},{11,3},{4,12},{12,4},... | collective-permute-start | bytes 184328 | tf_op jit(solution)/shard_map/ppermute | solution.py:14
  67.7 13.2 %collective-permute-start.5 = (bf16[160,768]{1,0:T(8,128)(2,1)S(1)}, bf16[160,768]{1,0:T(8,128)(2,1)S(1)}, u32[]{:S(2)}, u32[]{:S(2)}) collective-permute-start(bf16[160,768]{1,0:T(8,128)(2,1)S(1)} %slice.55), channel_id=1, source_target_pairs={{0,384},{128,0},{256,128},{384,256},{1,385},{129,1},{257,129},{385... | collective-permute-start | bytes 737288 | tf_op jit(solution)/shard_map/ppermute | solution.py:53
  70.9 10.0 %collective-permute-start.3 = (bf16[160,768]{1,0:T(8,128)(2,1)S(1)}, bf16[160,768]{1,0:T(8,128)(2,1)S(1)}, u32[]{:S(2)}, u32[]{:S(2)}) collective-permute-start(bf16[160,768]{1,0:T(8,128)(2,1)S(1)} %slice.54), channel_id=1, source_target_pairs={{0,128},{128,256},{256,384},{384,0},{1,129},{129,257},{257,385},{3... | collective-permute-start | bytes 737288 | tf_op jit(solution)/shard_map/ppermute | solution.py:53
  73.1 16.2 %collective-permute-start.10 = (bf16[2,2,40,384]{3,2,1,0:T(8,128)(2,1)S(1)}, bf16[2,2,40,384]{3,2,1,0:T(8,128)(2,1)S(1)}, u32[]{:S(2)}, u32[]{:S(2)}) collective-permute-start(bf16[2,2,40,384]{3,2,1,0:T(8,128)(2,1)S(1)} %get-tuple-element.43), channel_id=1, source_target_pairs={{0,6},{2,0},{4,2},{6,4},{1,7},{3,1},{5,3},{7,5},{8,14},{10,8},{12,... | collective-permute-start | bytes 368648 | tf_op jit(solution)/shard_map/ppermute | solution.py:53
  75.6 13.7 %collective-permute-start.9 = (bf16[2,2,40,384]{3,2,1,0:T(8,128)(2,1)S(1)}, bf16[2,2,40,384]{3,2,1,0:T(8,128)(2,1)}, u32[]{:S(2)}, u32[]{:S(2)}) collective-permute-start(bf16[2,2,40,384]{3,2,1,0:T(8,128)(2,1)S(1)} %get-tuple-element.43), channel_id=1, source_target_pairs={{0,4},{2,6},{4,0},{6,2},{1,5},{3,7},{5,1},{7,3},{8,12},{10,14},{12... | collective-permute-start | bytes 368648 | tf_op jit(solution)/shard_map/ppermute | solution.py:53
  79.0 10.3 %collective-permute-start.8 = (bf16[2,2,40,384]{3,2,1,0:T(8,128)(2,1)S(1)}, bf16[2,2,40,384]{3,2,1,0:T(8,128)(2,1)}, u32[]{:S(2)}, u32[]{:S(2)}) collective-permute-start(bf16[2,2,40,384]{3,2,1,0:T(8,128)(2,1)S(1)} %get-tuple-element.43), channel_id=1, source_target_pairs={{0,2},{2,4},{4,6},{6,0},{1,3},{3,5},{5,7},{7,1},{8,10},{10,12},{12... | collective-permute-start | bytes 368648 | tf_op jit(solution)/shard_map/ppermute | solution.py:53
  81.5 1.3 copy-start.1
  82.8 7.9 %collective-permute-start.6 = (bf16[640,384]{0,1:T(8,128)(2,1)S(1)}, bf16[640,384]{0,1:T(8,128)(2,1)S(1)}, u32[]{:S(2)}, u32[]{:S(2)}) collective-permute-start(bf16[640,384]{0,1:T(8,128)(2,1)S(1)} %fusion), channel_id=1, source_target_pairs={{0,1},{1,0},{2,3},{3,2},{4,5},{5,4},{6,7},{7,6},{8,9},{9,8},{10,11... | collective-permute-start | bytes 1474568 | tf_op jit(solution)/shard_map/ppermute | solution.py:14
  89.3 1.7 %copy-start.2 = (bf16[1280,768]{1,0:T(8,128)(2,1)S(1)}, bf16[1280,768]{1,0:T(8,128)(2,1)}, u32[]{:S(2)}) copy-start(bf16[1280,768]{1,0:T(8,128)(2,1)} %copy-done.1) | copy-start | bytes 5898244
  93.5 16.7 %all-to-all-start = ((bf16[16,2,12,384]{3,1,2,0:T(2,128)(2,1)}), bf16[16,2,12,384]{3,1,2,0:T(2,128)(2,1)S(1)}, u32[]{:S(2)}, u32[]{:S(2)}) async-start(bf16[16,2,12,384]{3,1,2,0:T(2,128)(2,1)} %bitcast.27), calls=%async_computation | async-start | bytes 589824 | tf_op jit(solution)/shard_map/all_to_all | solution.py:100
  99.8 49.5 %copy-start.3 = (f32[2,12,384]{2,0,1:T(2,128)S(1)}, f32[2,12,384]{2,0,1:T(2,128)}, u32[]{:S(2)}) copy-start(f32[2,12,384]{2,0,1:T(2,128)} %param.7) | copy-start | bytes 110596
  99.8 10.7 %collective-permute-start.11 = (bf16[2,80,384]{2,1,0:T(8,128)(2,1)S(1)}, bf16[2,80,384]{2,1,0:T(8,128)(2,1)S(1)}, u32[]{:S(2)}, u32[]{:S(2)}) collective-permute-start(bf16[2,80,384]{2,1,0:T(8,128)(2,1)S(1)} %get-tuple-element.34), channel_id=1, source_target_pairs={{0,2},{2,4},{4,6},{6,0},{1,3},{3,5},{5,7},{7,1},{8,10},{10,12},{12... | collective-permute-start | bytes 368648 | tf_op jit(solution)/shard_map/ppermute | solution.py:53
  102.3 8.2 %collective-permute-start.12 = (bf16[2,80,384]{2,1,0:T(8,128)(2,1)S(1)}, bf16[2,80,384]{2,1,0:T(8,128)(2,1)S(1)}, u32[]{:S(2)}, u32[]{:S(2)}) collective-permute-start(bf16[2,80,384]{2,1,0:T(8,128)(2,1)S(1)} %get-tuple-element.33), channel_id=1, source_target_pairs={{0,6},{2,0},{4,2},{6,4},{1,7},{3,1},{5,3},{7,5},{8,14},{10,8},{12,... | collective-permute-start | bytes 368648 | tf_op jit(solution)/shard_map/ppermute | solution.py:53
  106.3 7.1 %collective-permute-start.13 = (bf16[2,80,384]{2,1,0:T(8,128)(2,1)S(1)}, bf16[2,80,384]{2,1,0:T(8,128)(2,1)S(1)}, u32[]{:S(2)}, u32[]{:S(2)}) collective-permute-start(bf16[2,80,384]{2,1,0:T(8,128)(2,1)S(1)} %get-tuple-element.32), channel_id=1, source_target_pairs={{0,4},{2,6},{4,0},{6,2},{1,5},{3,7},{5,1},{7,3},{8,12},{10,14},{12... | collective-permute-start | bytes 368648 | tf_op jit(solution)/shard_map/ppermute | solution.py:53
  113.5 12.9 %collective-permute-start.14 = (bf16[2,40,384]{2,1,0:T(8,128)(2,1)S(1)}, bf16[2,40,384]{2,1,0:T(8,128)(2,1)S(1)}, u32[]{:S(2)}, u32[]{:S(2)}) collective-permute-start(bf16[2,40,384]{2,1,0:T(8,128)(2,1)S(1)} %select_bitcast_fusion), channel_id=1, source_target_pairs={{0,1},{1,0},{2,3},{3,2},{4,5},{5,4},{6,7},{7,6},{8,9},{9,8},{10,11... | collective-permute-start | bytes 184328 | tf_op jit(solution)/shard_map/ppermute | solution.py:14
  118.7 19.9 %all-to-all-start.1 = ((bf16[4,12,384]{2,1,0:T(8,128)(2,1)}), bf16[4,12,384]{2,1,0:T(8,128)(2,1)S(1)}, u32[]{:S(2)}, u32[]{:S(2)}) async-start(bf16[4,12,384]{2,1,0:T(8,128)(2,1)} %bitcast.39), calls=%async_computation.1 | async-start | bytes 98304 | tf_op jit(solution)/shard_map/all_to_all | solution.py:113
  126.5 17.6 %collective-permute-start.15 = (bf16[2,40,384]{2,1,0:T(8,128)(2,1)S(1)}, bf16[2,40,384]{2,1,0:T(8,128)(2,1)S(1)}, u32[]{:S(2)}, u32[]{:S(2)}) collective-permute-start(bf16[2,40,384]{2,1,0:T(8,128)(2,1)S(1)} %fusion.5), channel_id=1, source_target_pairs={{0,8},{8,0},{1,9},{9,1},{2,10},{10,2},{3,11},{11,3},{4,12},{12,4},... | collective-permute-start | bytes 184328 | tf_op jit(solution)/shard_map/ppermute | solution.py:14
  139.3 9.9 %all-to-all-start.2 = ((bf16[8,12,384]{2,1,0:T(8,128)(2,1)}), bf16[8,12,384]{2,1,0:T(8,128)(2,1)S(1)}, u32[]{:S(2)}, u32[]{:S(2)}) async-start(bf16[8,12,384]{2,1,0:T(8,128)(2,1)} %broadcast_in_dim.46), calls=%async_computation.2 | async-start | bytes 196608 | tf_op jit(solution)/shard_map/all_to_all | solution.py:27
